TPU v7x, 32 devices: a whole 2x2x4 slice. The times are simulated.
32 devices in a mesh: stream: 8 (over y, x, core), cross: 4 (over z).
Axes of the slice: x: 2, y: 2, z: 4, core: 2. Of those that a mesh axis runs over, the one named last changes fastest.
Arguments:
- initial_state: float32 [5, 64, 32768], P(None, 'stream', 'cross'), may hold values from -6 to 6
- forcing: float32 [5, 64, 32768], P(None, 'stream', 'cross'), may hold values from -0.3 to 0.3
- block_inverse: float32 [5, 5, 64, 32768], P(None, None, 'stream', 'cross'), may hold values from -1 to 1, as said below
- lower_decay: float32 [5, 64, 32768], P(None, 'stream', 'cross'), may hold values from 0 to 1
- upper_decay: float32 [5, 64, 32768], P(None, 'stream', 'cross'), may hold values from 0 to 1
- cross_coupling: float32 [64, 32768], P('stream', 'cross'), may hold values from 0.002 to 0.02
- iblank: int32 [64, 32768], P('stream', 'cross'), may hold values 0 or 1
- donor_receiver: int32 [1024, 1], P(('stream', 'cross')), may hold values from 0 to 31; in each aligned block of 32 rows (0 to 31, 32 to 63, ...) at most 2 rows name the same one
- donor_block: int32 [1024], P(('stream', 'cross')), may hold values from 0 to 511
- stencil_offset: int32 [1024], P(('stream', 'cross')), may hold values from 1 to 127
- stencil_weight: float32 [1024, 128], P(('stream', 'cross')), may hold values from 0.005 to 0.02
- fringe_target: int32 [2048], P(('stream', 'cross')), may hold values from 0 to 511
Outputs:
- final_state: float32 [5, 64, 32768], P(None, 'stream', 'cross')
- last_update: float32 [5, 64, 32768], P(None, 'stream', 'cross')
Inputs may be any that keep to these rules, and one draw needn't show every extreme that they name: `donor_receiver`: within the rows of one device no receiving device is named more than 2 times. `block_inverse`: each 5 x 5 block is orthogonal and symmetric.
All inputs are finite; a program needn't handle non-finite values. No bound on the sum of `iblank` on one device may be relied on, other than what follows from the above.
Results may differ from a plain program's by a relative error of at most 0.00018.
Values sent between devices are 32-bit elements; how exact they have to be, the bound alone decides.
A program may use at most 128 MiB of HBM per device.

v0:
```python
import functools

import jax
import jax.numpy as jnp
from jax import lax
from jax.experimental import pallas as pl
from jax.experimental.pallas import tpu as pltpu
from jax.sharding import PartitionSpec as P

ITERS = 2
CAP = 2
NV = 5
SLOT_ROWS = 16
STEP = 16
CHUNKS = 4
MESH = pl.DeviceIdType.MESH
PAIRS = [(a, b) for a in range(NV) for b in range(a, NV)]


def pair(a, b):
    return PAIRS.index((min(a, b), max(a, b)))


def split3(x):
    high = x.astype(jnp.bfloat16)
    rest = x - high.astype(jnp.float32)
    mid = rest.astype(jnp.bfloat16)
    low = (rest - mid.astype(jnp.float32)).astype(jnp.bfloat16)
    return jnp.concatenate([high, mid, low], axis=0)


def iota(shape, dim):
    return lax.broadcasted_iota(jnp.int32, shape, dim)


def kernel(
    ns, nc, planes, tiles,
    state_h, forcing_h, inverse_h, lower_h, upper_h, coupling_h, blank_h,
    receiver_r, block_s, offset_r, weight_r, target_r,
    final_h, update_h,
    state, forcing, inverse, lower, upper, coupling, blank,
    near, update, gathered, placed, outgoing, received, pick, stacked,
    edge_out, edge_in, face,
    load_sem, out_sem, own_sem, fsend, frecv, esend, erecv, wsend, wrecv,
):
    s, c = lax.axis_index("stream"), lax.axis_index("cross")
    devices = ns * nc
    me = s * nc + c
    senders = block_s.shape[0]
    slots = devices * CAP
    span = tiles // CHUNKS

    loads = []

    def load(source, target):
        copy = pltpu.make_async_copy(source, target, load_sem.at[len(loads)])
        copy.start()
        loads.append(copy)
        return copy

    def rows_of(i):
        return pl.ds(i * tiles, tiles)

    state_loads = [load(state_h.at[:, :, i, :], state.at[:, rows_of(i), :]) for i in range(planes)]
    drive_loads = []
    for i in range(planes):
        drive_loads.append(load(forcing_h.at[:, :, i, :], forcing.at[:, rows_of(i), :]))
        drive_loads.append(load(coupling_h.at[:, i, :], coupling.at[rows_of(i), :]))
        drive_loads.append(load(blank_h.at[:, i, :], blank.at[rows_of(i), :]))
    sweep_loads = []
    for i in range(planes):
        sweep_loads.append(load(lower_h.at[:, :, i, :], lower.at[:, rows_of(i), :]))
        for a in range(NV):
            first = pair(a, a)
            sweep_loads.append(
                load(
                    inverse_h.at[a, pl.ds(a, NV - a), :, i, :],
                    inverse.at[pl.ds(first, NV - a), rows_of(i), :],
                )
            )
    for i in range(planes):
        sweep_loads.append(load(upper_h.at[:, :, i, :], upper.at[:, rows_of(i), :]))

    barrier = pltpu.get_barrier_semaphore()

    def greet(k, carry):
        other = lax.rem(me + k, devices)
        pl.semaphore_signal(
            barrier, inc=1, device_id=(other // nc, lax.rem(other, nc)), device_id_type=MESH
        )
        return carry

    lax.fori_loop(1, devices, greet, 0)

    eye = iota((senders, senders), 0) == iota((senders, senders), 1)
    recv_row = receiver_r[...].astype(jnp.float32)
    recv_col = jnp.sum(jnp.where(eye, recv_row, 0.0), axis=1, keepdims=True)
    earlier = iota((senders, senders), 0) < iota((senders, senders), 1)
    rank_row = jnp.sum(
        jnp.where(earlier & (recv_col == recv_row), 1.0, 0.0), axis=0, keepdims=True
    )
    key_row = rank_row * devices + recv_row
    place = (key_row == iota((slots, senders), 0).astype(jnp.float32)).astype(jnp.float32)
    place3 = jnp.concatenate([place, place, place], axis=1).astype(jnp.bfloat16)
    offset_col = jnp.sum(
        jnp.where(eye, offset_r[...].astype(jnp.float32), 0.0), axis=1, keepdims=True
    ).astype(jnp.int32)
    offset_all = jnp.broadcast_to(offset_col, (senders, 128))

    slot_eye = iota((slots, slots), 0) == iota((slots, slots), 1)
    target_col = jnp.sum(
        jnp.where(slot_eye, target_r[...].astype(jnp.float32), 0.0), axis=1, keepdims=True
    )
    slot_k = iota((slots, slots), 1)
    wanted = jnp.where(slot_k < devices, slot_k * CAP, (slot_k - devices) * CAP + 1)
    target_row = jnp.sum(
        jnp.where(iota((slots, slots), 0) == wanted, target_col, 0.0), axis=0, keepdims=True
    )
    target3 = jnp.concatenate([target_row, target_row, target_row], axis=1)

    def fill(i, carry):
        ids = (iota((tiles, 3 * slots), 0) + i * tiles).astype(jnp.float32)
        pick[pl.ds(pl.multiple_of(i * tiles, tiles), tiles), :] = jnp.where(
            ids == target3, 1.0, 0.0
        ).astype(jnp.bfloat16)
        return carry

    lax.fori_loop(0, planes, fill, 0)
    for it in range(ITERS):
        for r in range(NV * CAP, SLOT_ROWS):
            outgoing[it, pl.ds(r, devices, stride=SLOT_ROWS), :] = jnp.zeros(
                (devices, 128), jnp.float32
            )

    for copy in state_loads:
        copy.wait()
    pl.semaphore_wait(barrier, devices - 1)

    def fringe_copy(it, k):
        other = lax.rem(me + k, devices)
        start = pl.multiple_of(other * SLOT_ROWS, SLOT_ROWS)
        mine = pl.multiple_of(me * SLOT_ROWS, SLOT_ROWS)
        return pltpu.make_async_remote_copy(
            src_ref=outgoing.at[it, pl.ds(start, SLOT_ROWS), :],
            dst_ref=received.at[it, pl.ds(mine, SLOT_ROWS), :],
            send_sem=fsend.at[it, k],
            recv_sem=frecv.at[it, k],
            device_id=(other // nc, lax.rem(other, nc)),
            device_id_type=MESH,
        )

    def edge_copy(it, side):
        other = lax.rem(c + 1, nc) if side == 0 else lax.rem(c + nc - 1, nc)
        return pltpu.make_async_remote_copy(
            src_ref=edge_out.at[it, side],
            dst_ref=edge_in.at[it, side],
            send_sem=esend.at[it, side],
            recv_sem=erecv.at[it, side],
            device_id=(s, other),
            device_id_type=MESH,
        )

    def wave_copy(it, down, part):
        rows = pl.ds(part * span, span)
        if down:
            source = near.at[:, pl.ds((planes - 1) * tiles + part * span, span), :]
            other = lax.rem(s + 1, ns)
        else:
            source = update.at[:, rows, :]
            other = lax.rem(s + ns - 1, ns)
        way = 0 if down else 1
        return pltpu.make_async_remote_copy(
            src_ref=source,
            dst_ref=face.at[it, way, :, rows, :],
            send_sem=wsend.at[it, way, part],
            recv_sem=wrecv.at[it, way, part],
            device_id=(other, c),
            device_id_type=MESH,
        )

    def start_face(it, way, part):
        at_end = (s == 0) if way == 0 else (s == ns - 1)

        @pl.when(at_end)
        def _():
            face[it, way, :, pl.ds(part * span, span), :] = jnp.zeros(
                (NV, span, 128), jnp.float32
            )

        @pl.when(jnp.logical_not(at_end))
        def _():
            wave_copy(it, way == 0, part).wait_recv()

    def apply(rows, vector):
        out = []
        for a in range(NV):
            total = None
            for b in range(NV):
                term = inverse[pair(a, b), rows, :] * vector[b]
                total = term if total is None else total + term
            out.append(total)
        return out

    def sweep_down(it, part):
        start_face(it, 0, part)

        def step(g, carry):
            base = part * span + g * STEP
            x = [face[it, 0, v, pl.ds(base, STEP), :] for v in range(NV)]
            for i in range(planes):
                rows = pl.ds(i * tiles + base, STEP)
                t = [near[v, rows, :] + lower[v, rows, :] * x[v] for v in range(NV)]
                x = apply(rows, t)
                for v in range(NV):
                    near[v, rows, :] = x[v]
            return carry

        for g in range(span // STEP):
            step(g, 0)

        @pl.when(s < ns - 1)
        def _():
            wave_copy(it, True, part).start()

    def out_copies(part):
        copies = []
        for i in range(planes):
            rows = pl.ds(i * tiles + part * span, span)
            for n, (source, target) in enumerate(((state, final_h), (update, update_h))):
                copies.append(
                    pltpu.make_async_copy(
                        source.at[:, rows, :],
                        target.at[:, pl.ds(part * span, span), i, :],
                        out_sem.at[part, i, n],
                    )
                )
        return copies

    def sweep_up(it, part):
        start_face(it, 1, part)

        def step(g, carry):
            base = part * span + g * STEP
            y = [face[it, 1, v, pl.ds(base, STEP), :] for v in range(NV)]
            for i in reversed(range(planes)):
                rows = pl.ds(i * tiles + base, STEP)
                t = [upper[v, rows, :] * y[v] for v in range(NV)]
                z = apply(rows, t)
                y = [near[v, rows, :] + z[v] for v in range(NV)]
                for v in range(NV):
                    update[v, rows, :] = y[v]
                    state[v, rows, :] = state[v, rows, :] + y[v]
            return carry

        for g in range(span // STEP):
            step(g, 0)

        @pl.when(s > 0)
        def _():
            wave_copy(it, False, part).start()

        if it == ITERS - 1:
            for copy in out_copies(part):
                copy.start()

    for it in range(ITERS):
        for v in range(NV):
            edge_out[it, 0, v] = state[v, pl.ds(tiles - 1, planes, stride=tiles), :]
            edge_out[it, 1, v] = state[v, pl.ds(0, planes, stride=tiles), :]
        for side in range(2):
            edge_copy(it, side).start()

        def gather(q, carry):
            for k in range(8):
                e = q * 8 + k
                block = block_s[e]
                for v in range(NV):
                    gathered[v, pl.ds(e, 1), :] = state[v, pl.ds(block, 1), :]
            return carry

        lax.fori_loop(0, senders // 8, gather, 0)
        weight = weight_r[...]
        for v in range(NV):
            chosen = gathered[v]
            moved = chosen
            for bit in range(7):
                rolled = pltpu.roll(moved, 128 - (1 << bit), 1)
                moved = jnp.where((offset_all & (1 << bit)) != 0, rolled, moved)
            placed[:, v * 128:(v + 1) * 128] = split3(weight * (chosen + moved))
        slot_values = jnp.dot(place3, placed[...], preferred_element_type=jnp.float32)
        for v in range(NV):
            for k in range(CAP):
                outgoing[it, pl.ds(v * CAP + k, devices, stride=SLOT_ROWS), :] = slot_values[
                    k * devices:(k + 1) * devices, v * 128:(v + 1) * 128
                ]

        def send(k, carry):
            fringe_copy(it, k).start()
            return carry

        lax.fori_loop(1, devices, send, 0)
        mine = pl.ds(pl.multiple_of(me * SLOT_ROWS, SLOT_ROWS), SLOT_ROWS)
        received[it, mine, :] = outgoing[it, mine, :]

        if it == 0:
            for copy in drive_loads:
                copy.wait()
        else:
            for part in range(CHUNKS):
                @pl.when(s < ns - 1)
                def _():
                    wave_copy(it - 1, True, part).wait_send()

                @pl.when(s > 0)
                def _():
                    wave_copy(it - 1, False, part).wait_send()
        for side in range(2):
            edge_copy(it, side).wait_recv()
        lane = iota((tiles, 128), 1)
        row = iota((tiles, 128), 0)

        def drive(i, carry):
            rows = pl.ds(pl.multiple_of(i * tiles, tiles), tiles)
            factor = coupling[rows, :]
            for v in range(NV):
                x = state[v, rows, :]
                before = pltpu.roll(edge_in[it, 0, v, pl.ds(i, 1), :], 1, 1)
                after = pltpu.roll(edge_in[it, 1, v, pl.ds(i, 1), :], 127, 1)
                left = pltpu.roll(x, 1, 1)
                left = jnp.where(
                    lane == 0, jnp.where(row == 0, before, pltpu.roll(left, 1, 0)), left
                )
                right = pltpu.roll(x, 127, 1)
                right = jnp.where(
                    lane == 127,
                    jnp.where(row == tiles - 1, after, pltpu.roll(right, tiles - 1, 0)),
                    right,
                )
                near[v, rows, :] = forcing[v, rows, :] - factor * (2.0 * x - left - right)
            return carry

        lax.fori_loop(0, planes, drive, 0)

        def take(k, carry):
            fringe_copy(it, k).wait_recv()
            return carry

        lax.fori_loop(1, devices, take, 0)
        for v in range(NV):
            parts = [
                received[it, pl.ds(v * CAP + k, devices, stride=SLOT_ROWS), :] for k in range(CAP)
            ]
            stacked[:, v * 128:(v + 1) * 128] = split3(jnp.concatenate(parts, axis=0))

        def add_fringe(i, carry):
            rows = pl.ds(pl.multiple_of(i * tiles, tiles), tiles)
            hole = (1 - blank[rows, :]).astype(jnp.float32)
            fringe = jnp.dot(pick[rows, :], stacked[...], preferred_element_type=jnp.float32)
            for v in range(NV):
                near[v, rows, :] = near[v, rows, :] + hole * fringe[:, v * 128:(v + 1) * 128]
            return carry

        lax.fori_loop(0, planes, add_fringe, 0)

        if it == 0:
            for copy in sweep_loads:
                copy.wait()
        for part in range(CHUNKS):
            sweep_down(it, part)

            @pl.when(s == ns - 1)
            def _():
                sweep_up(it, part)

        @pl.when(s < ns - 1)
        def _():
            for part in range(CHUNKS):
                sweep_up(it, part)

        for side in range(2):
            edge_copy(it, side).wait_send()

        def sent(k, carry):
            fringe_copy(it, k).wait_send()
            return carry

        lax.fori_loop(1, devices, sent, 0)

    for part in range(CHUNKS):
        @pl.when(s < ns - 1)
        def _():
            wave_copy(ITERS - 1, True, part).wait_send()

        @pl.when(s > 0)
        def _():
            wave_copy(ITERS - 1, False, part).wait_send()

        for copy in out_copies(part):
            copy.wait()


def shards(
    initial_state, forcing, block_inverse, lower_decay, upper_decay, cross_coupling, iblank,
    donor_receiver, donor_block, stencil_offset, stencil_weight, fringe_target,
):
    ns, nc = lax.axis_size("stream"), lax.axis_size("cross")
    devices = ns * nc
    planes, cells = initial_state.shape[1:]
    tiles = cells // 128
    senders = donor_block.shape[0]
    slots = devices * CAP

    def tiled(x):
        lead = x.shape[:-2]
        n = len(lead)
        order = tuple(range(n)) + (n + 1, n, n + 2)
        return x.reshape(lead + (planes, tiles, 128)).transpose(order)

    def untiled(x):
        return x.transpose(0, 2, 1, 3).reshape(NV, planes, cells)

    full = (NV, planes * tiles, 128)
    f32, bf16 = jnp.float32, jnp.bfloat16
    dma = pltpu.SemaphoreType.DMA
    out = jax.ShapeDtypeStruct((NV, tiles, planes, 128), f32)
    hbm = pl.BlockSpec(memory_space=pl.ANY)
    vmem = pl.BlockSpec(memory_space=pltpu.VMEM)
    smem = pl.BlockSpec(memory_space=pltpu.SMEM)
    final, update = pl.pallas_call(
        functools.partial(kernel, ns, nc, planes, tiles),
        out_shape=(out, out),
        in_specs=[hbm] * 7 + [vmem, smem, vmem, vmem, vmem],
        out_specs=(hbm, hbm),
        scratch_shapes=[
            pltpu.VMEM(full, f32),
            pltpu.VMEM(full, f32),
            pltpu.VMEM((len(PAIRS),) + full[1:], f32),
            pltpu.VMEM(full, f32),
            pltpu.VMEM(full, f32),
            pltpu.VMEM(full[1:], f32),
            pltpu.VMEM(full[1:], jnp.int32),
            pltpu.VMEM(full, f32),
            pltpu.VMEM(full, f32),
            pltpu.VMEM((NV, senders, 128), f32),
            pltpu.VMEM((3 * senders, NV * 128), bf16),
            pltpu.VMEM((ITERS, devices * SLOT_ROWS, 128), f32),
            pltpu.VMEM((ITERS, devices * SLOT_ROWS, 128), f32),
            pltpu.VMEM((planes * tiles, 3 * slots), bf16),
            pltpu.VMEM((3 * slots, NV * 128), bf16),
            pltpu.VMEM((ITERS, 2, NV, planes, 128), f32),
            pltpu.VMEM((ITERS, 2, NV, planes, 128), f32),
            pltpu.VMEM((ITERS, 2, NV, tiles, 128), f32),
            dma((planes * (4 + 2 + NV),)),
            dma((CHUNKS, planes, 2)),
            dma((1,)),
            dma((ITERS, devices)),
            dma((ITERS, devices)),
            dma((ITERS, 2)),
            dma((ITERS, 2)),
            dma((ITERS, 2, CHUNKS)),
            dma((ITERS, 2, CHUNKS)),
        ],
        compiler_params=pltpu.CompilerParams(
            collective_id=0, has_side_effects=True, vmem_limit_bytes=56 * 1024 * 1024
        ),
    )(
        tiled(initial_state), tiled(forcing), tiled(block_inverse), tiled(lower_decay),
        tiled(upper_decay), tiled(cross_coupling), tiled(iblank),
        donor_receiver.reshape(1, senders), donor_block, stencil_offset.reshape(1, senders), stencil_weight,
        fringe_target.reshape(1, slots),
    )
    return untiled(final), untiled(update)


def solution(mesh):
    return jax.shard_map(
        shards,
        mesh=mesh,
        in_specs=(
            P(None, "stream", "cross"),
            P(None, "stream", "cross"),
            P(None, None, "stream", "cross"),
            P(None, "stream", "cross"),
            P(None, "stream", "cross"),
            P("stream", "cross"),
            P("stream", "cross"),
            P(("stream", "cross"), None),
            P(("stream", "cross")),
            P(("stream", "cross")),
            P(("stream", "cross"), None),
            P(("stream", "cross")),
        ),
        out_specs=(P(None, "stream", "cross"), P(None, "stream", "cross")),
        check_vma=False,
    )
```

profile of v0, /device:TPU:0, one launch (start us, length us, event | category | flops | bytes accessed | tf_op | source)
XLA Modules:
  0.0 95.1 jit_solution(903783582264383177)
XLA Ops:
  0.6 90.8 %shard_map.131 = (f32[5,64,8,128]{3,2,1,0:T(8,128)}, f32[5,64,8,128]{3,2,1,0:T(8,128)}) custom-call(f32[5,64,8,128]{3,2,1,0:T(8,128)} %bitcast.31, f32[5,64,8,128]{3,2,1,0:T(8,128)} %bitcast.32, f32[5,5,64,8,128]{4,3,2,1,0:T(8,128)} %bitcast.30, f32[5,64,8,128]{3,2,1,0:T(8,128)} %bitcast.33, f32[5,64,8,128]{3,2,1,0:T(8,128)} %bitcast.34, ...), custom_call_target="tpu_custom_call" | custom-call | tf_op jit(solution)/shard_map/pallas_call | solution.py:429
  91.5 0.0 copy-start
  91.5 2.6 %copy.16 = f32[5,8,8192]{2,1,0:T(8,128)} copy(f32[5,8,8192]{2,1,0:T(8,128)} %bitcast.36) | data formatting | bytes 2621440
  94.0 0.0 copy-done
  94.0 1.1 %copy.17 = f32[5,8,8192]{2,1,0:T(8,128)} copy(f32[5,8,8192]{2,1,0:T(8,128)S(1)} %bitcast.35) | data formatting | bytes 2621440
Async XLA Ops:
  91.5 2.6 %copy-start = (f32[5,64,8,128]{3,2,1,0:T(8,128)S(1)}, f32[5,64,8,128]{3,2,1,0:T(8,128)}, u32[]{:S(2)}) copy-start(f32[5,64,8,128]{3,2,1,0:T(8,128)} %get-tuple-element.5) | copy-start | bytes 3932164
where the time goes:
time: 95.3 us; the launch traced here: 95.1 us
  Pallas kernels  90.8 us (95%)
  local copies, waits for them, and re-layouts  3.62 us (4%)
    pallas_call x1, Pallas kernels, shards(): pl.pallas_call(functools.partial(kernel, ns, nc, planes, tiles), out_shap...  90.8 us
    unnamed x4, local copies, waits for them, and re-layouts  3.62 us

commit v1 on v0

v1 whole, which is shorter than its diff:
```python
import functools

import jax
import jax.numpy as jnp
from jax import lax
from jax.experimental import pallas as pl
from jax.experimental.pallas import tpu as pltpu
from jax.sharding import PartitionSpec as P

ITERS = 2
CAP = 2
NV = 5
SLOT_ROWS = 16
STEP = 16
MATS = NV * NV
MESH = pl.DeviceIdType.MESH
PAIRS = [(a, b) for a in range(NV) for b in range(a, NV)]


def pair(a, b):
    return PAIRS.index((min(a, b), max(a, b)))


def split3(x):
    high = x.astype(jnp.bfloat16)
    rest = x - high.astype(jnp.float32)
    mid = rest.astype(jnp.bfloat16)
    low = (rest - mid.astype(jnp.float32)).astype(jnp.bfloat16)
    return jnp.concatenate([high, mid, low], axis=0)


def iota(shape, dim):
    return lax.broadcasted_iota(jnp.int32, shape, dim)


def kernel(
    ns, nc, planes, tiles,
    state_h, forcing_h, inverse_h, lower_h, upper_h, coupling_h, blank_h,
    receiver_r, block_s, offset_r, weight_r, target_r,
    final_h, update_h,
    state, forcing, inverse, lower, upper, coupling, blank,
    drive, near, update, gathered, placed, outgoing, received, pick, stacked,
    edge_out, edge_in,
    stage, mats, comp, prev_a, next_e,
    zero, chip_b, chip_c, prev_b, x_in, x_out, x_face, g_own, g_in, y_in, y_out, y_face,
    load_sem, out_sem, fsend, frecv, esend, erecv, msend, mrecv, csend, crecv,
):
    s, c = lax.axis_index("stream"), lax.axis_index("cross")
    devices = ns * nc
    me = s * nc + c
    senders = block_s.shape[0]
    slots = devices * CAP
    groups = ns // 2
    half = tiles // 2
    core = lax.rem(s, 2)
    group = s // 2
    odd = lax.rem(group, 2) == 1
    own_base = lax.rem(core + group, 2) * half
    far_base = half - own_base

    loads = []

    def load(source, target):
        copy = pltpu.make_async_copy(source, target, load_sem.at[len(loads)])
        copy.start()
        loads.append(copy)
        return copy

    def rows_of(i):
        return pl.ds(i * tiles, tiles)

    state_loads = [load(state_h.at[:, :, i, :], state.at[:, rows_of(i), :]) for i in range(planes)]
    sweep_loads = []
    for i in range(planes):
        sweep_loads.append(load(lower_h.at[:, :, i, :], lower.at[:, rows_of(i), :]))
        for a in range(NV):
            first = pair(a, a)
            sweep_loads.append(
                load(
                    inverse_h.at[a, pl.ds(a, NV - a), :, i, :],
                    inverse.at[pl.ds(first, NV - a), rows_of(i), :],
                )
            )
    for i in range(planes):
        sweep_loads.append(load(upper_h.at[:, :, i, :], upper.at[:, rows_of(i), :]))
    drive_loads = []
    for i in range(planes):
        drive_loads.append(load(forcing_h.at[:, :, i, :], forcing.at[:, rows_of(i), :]))
        drive_loads.append(load(coupling_h.at[:, i, :], coupling.at[rows_of(i), :]))
        drive_loads.append(load(blank_h.at[:, i, :], blank.at[rows_of(i), :]))

    barrier = pltpu.get_barrier_semaphore()

    def greet(k, carry):
        other = lax.rem(me + k, devices)
        pl.semaphore_signal(
            barrier, inc=1, device_id=(other // nc, lax.rem(other, nc)), device_id_type=MESH
        )
        return carry

    lax.fori_loop(1, devices, greet, 0)

    eye = iota((senders, senders), 0) == iota((senders, senders), 1)
    recv_row = receiver_r[...].astype(jnp.float32)
    recv_col = jnp.sum(jnp.where(eye, recv_row, 0.0), axis=1, keepdims=True)
    earlier = iota((senders, senders), 0) < iota((senders, senders), 1)
    rank_row = jnp.sum(
        jnp.where(earlier & (recv_col == recv_row), 1.0, 0.0), axis=0, keepdims=True
    )
    key_row = rank_row * devices + recv_row
    place = (key_row == iota((slots, senders), 0).astype(jnp.float32)).astype(jnp.float32)
    place3 = jnp.concatenate([place, place, place], axis=1).astype(jnp.bfloat16)
    offset_col = jnp.sum(
        jnp.where(eye, offset_r[...].astype(jnp.float32), 0.0), axis=1, keepdims=True
    ).astype(jnp.int32)
    offset_all = jnp.broadcast_to(offset_col, (senders, 128))

    def fill_pick():
        slot_eye = iota((slots, slots), 0) == iota((slots, slots), 1)
        target_col = jnp.sum(
            jnp.where(slot_eye, target_r[...].astype(jnp.float32), 0.0), axis=1, keepdims=True
        )
        slot_k = iota((slots, slots), 1)
        wanted = jnp.where(slot_k < devices, slot_k * CAP, (slot_k - devices) * CAP + 1)
        target_row = jnp.sum(
            jnp.where(iota((slots, slots), 0) == wanted, target_col, 0.0), axis=0, keepdims=True
        )
        target3 = jnp.concatenate([target_row, target_row, target_row], axis=1)

        def fill(i, carry):
            ids = (iota((tiles, 3 * slots), 0) + i * tiles).astype(jnp.float32)
            pick[pl.ds(pl.multiple_of(i * tiles, tiles), tiles), :] = jnp.where(
                ids == target3, 1.0, 0.0
            ).astype(jnp.bfloat16)
            return carry

        lax.fori_loop(0, planes, fill, 0)

    for copy in state_loads:
        copy.wait()
    pl.semaphore_wait(barrier, devices - 1)

    def fringe_copy(it, k):
        other = lax.rem(me + k, devices)
        start = pl.multiple_of(other * SLOT_ROWS, SLOT_ROWS)
        mine = pl.multiple_of(me * SLOT_ROWS, SLOT_ROWS)
        return pltpu.make_async_remote_copy(
            src_ref=outgoing.at[it, pl.ds(start, NV * CAP), :],
            dst_ref=received.at[it, pl.ds(mine, NV * CAP), :],
            send_sem=fsend.at[it, k],
            recv_sem=frecv.at[it, k],
            device_id=(other // nc, lax.rem(other, nc)),
            device_id_type=MESH,
        )

    def edge_copy(it, side):
        other = lax.rem(c + 1, nc) if side == 0 else lax.rem(c + nc - 1, nc)
        return pltpu.make_async_remote_copy(
            src_ref=edge_out.at[it, side],
            dst_ref=edge_in.at[it, side],
            send_sem=esend.at[it, side],
            recv_sem=erecv.at[it, side],
            device_id=(s, other),
            device_id_type=MESH,
        )

    def member(other_group, across):
        return other_group * 2 + (1 - core if across else core)

    partner = member(group, True)

    def face_copy(it, kind, way, source, target, to):
        return pltpu.make_async_remote_copy(
            src_ref=source,
            dst_ref=target,
            send_sem=csend.at[it, way],
            recv_sem=crecv.at[it, kind],
            device_id=(to, c),
            device_id_type=MESH,
        )

    def mats_copy(k):
        third = pl.ds(k * MATS, MATS)
        return pltpu.make_async_remote_copy(
            src_ref=mats.at[2, third],
            dst_ref=mats.at[core, third],
            send_sem=msend.at[k],
            recv_sem=mrecv.at[k],
            device_id=(partner, c),
            device_id_type=MESH,
        )

    def prev_a_copy():
        return pltpu.make_async_remote_copy(
            src_ref=comp.at[pl.ds(0, MATS)],
            dst_ref=prev_a,
            send_sem=msend.at[3],
            recv_sem=mrecv.at[3],
            device_id=(member(group + 1, True), c),
            device_id_type=MESH,
        )

    def next_e_copy():
        return pltpu.make_async_remote_copy(
            src_ref=comp.at[pl.ds(MATS, MATS)],
            dst_ref=next_e,
            send_sem=msend.at[4],
            recv_sem=mrecv.at[4],
            device_id=(member(group - 1, True), c),
            device_id_type=MESH,
        )

    def b_to_partner(it):
        return face_copy(it, 0, 0, zero.at[it, 2, 0], zero.at[it, core, 0], partner)

    def c_to_partner(it):
        return face_copy(it, 1, 1, zero.at[it, 2, 1], zero.at[it, core, 1], partner)

    def b_to_next(it):
        return face_copy(it, 2, 2, chip_b.at[it], prev_b.at[it], member(group + 1, True))

    def x_to_next(it):
        return face_copy(it, 3, 3, x_out.at[it], x_in.at[it], member(group + 1, True))

    def x_to_skip(it):
        return face_copy(it, 3, 4, x_out.at[it], x_in.at[it], member(group + 2, False))

    def g_to_prev(it):
        return face_copy(it, 4, 5, g_own.at[it], g_in.at[it], member(group - 1, True))

    def y_to_prev(it):
        return face_copy(it, 5, 6, y_out.at[it], y_in.at[it], member(group - 1, True))

    def y_to_skip(it):
        return face_copy(it, 5, 7, y_out.at[it], y_in.at[it], member(group - 2, False))

    own_rows = pl.ds(pl.multiple_of(own_base, half), half)

    def x_to_partner(it):
        source = x_face.at[it, 1 - core, :, own_rows, :]
        return face_copy(it, 6, 8, source, source, partner)

    def y_to_partner(it):
        source = y_face.at[it, 1 - core, :, own_rows, :]
        return face_copy(it, 7, 9, source, source, partner)

    def block(rows):
        return [inverse[k, rows, :] for k in range(len(PAIRS))]

    def dot(terms):
        total = None
        for left, right in terms:
            total = left * right if total is None else total + left * right
        return total

    def apply(blocks, vector):
        return [dot([(blocks[pair(a, b)], vector[b]) for b in range(NV)]) for a in range(NV)]

    def at(base, size):
        return pl.ds(pl.multiple_of(base, 8), size)

    def matrix(ref, first, rows):
        return [[ref[first + a * NV + b, rows, :] for b in range(NV)] for a in range(NV)]

    def times(rows_of_matrix, vector):
        return [dot([(rows_of_matrix[a][b], vector[b]) for b in range(NV)]) for a in range(NV)]

    def column(m, b):
        return [m[a][b] for a in range(NV)]

    def transfer(q, carry):
        each = half // 8
        local = lax.rem(q, each) * 8
        base = jnp.where(q < each, far_base, own_base) + local
        slot = jnp.where(q < each, 2, core)
        spot = at(local, 8)
        chain = None
        for i in range(planes):
            rows = at(i * tiles + base, 8)
            blocks = block(rows)
            factor = [lower[v, rows, :] for v in range(NV)]
            if i == 0:
                chain = [[blocks[pair(a, b)] * factor[b] for a in range(NV)] for b in range(NV)]
            else:
                chain = [
                    apply(blocks, [factor[v] * chain[b][v] for v in range(NV)]) for b in range(NV)
                ]
            for b in range(NV):
                for a in range(NV):
                    stage[i, a * NV + b] = chain[b][a]
        for b in range(NV):
            for a in range(NV):
                mats[slot, a * NV + b, spot, :] = chain[b][a]
        both = chain
        for i in reversed(range(planes - 1)):
            rows = at(i * tiles + base, 8)
            blocks = block(rows)
            factor = [upper[v, rows, :] for v in range(NV)]
            both = [
                [
                    stage[i, a * NV + b] + z
                    for a, z in enumerate(apply(blocks, [factor[v] * both[b][v] for v in range(NV)]))
                ]
                for b in range(NV)
            ]
        for b in range(NV):
            for a in range(NV):
                mats[slot, 2 * MATS + a * NV + b, spot, :] = both[b][a]
        back = None
        for i in reversed(range(planes)):
            rows = at(i * tiles + base, 8)
            blocks = block(rows)
            factor = [upper[v, rows, :] for v in range(NV)]
            if i == planes - 1:
                back = [[blocks[pair(a, b)] * factor[b] for a in range(NV)] for b in range(NV)]
            else:
                back = [
                    apply(blocks, [factor[v] * back[b][v] for v in range(NV)]) for b in range(NV)
                ]
        for b in range(NV):
            for a in range(NV):
                mats[slot, MATS + a * NV + b, spot, :] = back[b][a]

        @pl.when(q == each - 1)
        def _():
            for k in range(3):
                mats_copy(k).start()

        return carry

    def compose(q, carry):
        rows = at(q * 8, 8)
        low_a = matrix(mats.at[0], 0, rows)
        high_a = matrix(mats.at[1], 0, rows)
        for b in range(NV):
            out = times(high_a, column(low_a, b))
            for a in range(NV):
                comp[a * NV + b, rows, :] = out[a]
        low_e = matrix(mats.at[0], MATS, rows)
        high_e = matrix(mats.at[1], MATS, rows)
        for b in range(NV):
            out = times(low_e, column(high_e, b))
            for a in range(NV):
                comp[MATS + a * NV + b, rows, :] = out[a]
        high_d = matrix(mats.at[1], 2 * MATS, rows)
        for b in range(NV):
            inner = times(high_d, column(low_a, b))
            out = times(low_e, inner)
            for a in range(NV):
                k = 2 * MATS + a * NV + b
                comp[k, rows, :] = mats[0, k, rows, :] + out[a]
        return carry

    def zero_down(it, base, slot):
        for g in range(half // STEP):
            x = None
            for i in range(planes):
                rows = at(i * tiles + base + g * STEP, STEP)
                t = [drive[v, rows, :] for v in range(NV)]
                if x is not None:
                    t = [t[v] + lower[v, rows, :] * x[v] for v in range(NV)]
                x = apply(block(rows), t)
                for v in range(NV):
                    near[v, rows, :] = x[v]
            for v in range(NV):
                zero[it, slot, 0, v, pl.ds(g * STEP, STEP), :] = x[v]

    def zero_up(it, base, slot):
        for g in range(half // STEP):
            rows = at((planes - 1) * tiles + base + g * STEP, STEP)
            y = [near[v, rows, :] for v in range(NV)]
            for i in reversed(range(planes - 1)):
                rows = at(i * tiles + base + g * STEP, STEP)
                z = apply(block(rows), [upper[v, rows, :] * y[v] for v in range(NV)])
                y = [near[v, rows, :] + z[v] for v in range(NV)]
            for v in range(NV):
                zero[it, slot, 1, v, pl.ds(g * STEP, STEP), :] = y[v]

    def true_down(it, base):
        for g in range(half // STEP):
            x = [x_face[it, core, v, at(base + g * STEP, STEP), :] for v in range(NV)]
            for i in range(planes):
                rows = at(i * tiles + base + g * STEP, STEP)
                t = [drive[v, rows, :] + lower[v, rows, :] * x[v] for v in range(NV)]
                x = apply(block(rows), t)
                for v in range(NV):
                    near[v, rows, :] = x[v]

    def true_up(it, base):
        for g in range(half // STEP):
            y = [y_face[it, core, v, at(base + g * STEP, STEP), :] for v in range(NV)]
            for i in reversed(range(planes)):
                rows = at(i * tiles + base + g * STEP, STEP)
                z = apply(block(rows), [upper[v, rows, :] * y[v] for v in range(NV)])
                y = [near[v, rows, :] + z[v] for v in range(NV)]
                for v in range(NV):
                    if it == ITERS - 1:
                        update[v, rows, :] = y[v]
                    state[v, rows, :] = state[v, rows, :] + y[v]

    def out_copies(part, base):
        copies = []
        for i in range(planes):
            rows = pl.ds(pl.multiple_of(i * tiles + base, half), half)
            cells = pl.ds(pl.multiple_of(base, half), half)
            for n, (source, target) in enumerate(((state, final_h), (update, update_h))):
                copies.append(
                    pltpu.make_async_copy(
                        source.at[:, rows, :], target.at[:, cells, i, :], out_sem.at[part, i, n]
                    )
                )
        return copies

    steps = [pl.ds(g * STEP, STEP) for g in range(half // STEP)]

    def chip_forward(it):
        for rows in steps:
            low = [zero[it, 0, 0, v, rows, :] for v in range(NV)]
            out = times(matrix(mats.at[1], 0, rows), low)
            for v in range(NV):
                chip_b[it, v, rows, :] = zero[it, 1, 0, v, rows, :] + out[v]

    def chip_backward(it):
        for rows in steps:
            low = [zero[it, 0, 0, v, rows, :] for v in range(NV)]
            out = times(matrix(mats.at[1], 2 * MATS, rows), low)
            out = [out[v] + zero[it, 1, 1, v, rows, :] for v in range(NV)]
            out = times(matrix(mats.at[0], MATS, rows), out)
            for v in range(NV):
                chip_c[it, v, rows, :] = zero[it, 0, 1, v, rows, :] + out[v]

    def own(g):
        return at(own_base + g * STEP, STEP)

    def relay_forward(it):
        for g, rows in enumerate(steps):
            out = times(matrix(prev_a, 0, rows), [x_in[it, v, rows, :] for v in range(NV)])
            x = [prev_b[it, v, rows, :] + out[v] for v in range(NV)]
            out = times(matrix(comp, 0, rows), x)
            for v in range(NV):
                x_out[it, v, rows, :] = chip_b[it, v, rows, :] + out[v]
                x_face[it, 0, v, own(g), :] = x[v]

    def turn(it):
        for g, rows in enumerate(steps):
            x = [x_face[it, 0, v, own(g), :] for v in range(NV)]
            out = times(matrix(comp, 2 * MATS, rows), x)
            for v in range(NV):
                g_own[it, v, rows, :] = chip_c[it, v, rows, :] + out[v]

    def inner_forward(it):
        for g, rows in enumerate(steps):
            x = [x_face[it, 0, v, own(g), :] for v in range(NV)]
            out = times(matrix(mats.at[0], 0, rows), x)
            for v in range(NV):
                x_face[it, 1, v, own(g), :] = zero[it, 0, 0, v, rows, :] + out[v]

    def relay_backward(it):
        for g, rows in enumerate(steps):
            out = times(matrix(next_e, 0, rows), [y_in[it, v, rows, :] for v in range(NV)])
            y = [g_in[it, v, rows, :] + out[v] for v in range(NV)]
            out = times(matrix(comp, MATS, rows), y)
            for v in range(NV):
                y_out[it, v, rows, :] = g_own[it, v, rows, :] + out[v]
                y_face[it, 1, v, own(g), :] = y[v]

    def inner_backward(it):
        for g, rows in enumerate(steps):
            x = [x_face[it, 1, v, own(g), :] for v in range(NV)]
            out = times(matrix(mats.at[1], 2 * MATS, rows), x)
            y = [y_face[it, 1, v, own(g), :] for v in range(NV)]
            back = times(matrix(mats.at[1], MATS, rows), y)
            for v in range(NV):
                y_face[it, 0, v, own(g), :] = zero[it, 1, 1, v, rows, :] + out[v] + back[v]

    face_zero = jnp.zeros((NV, half, 128), jnp.float32)

    @pl.when(group == 1)
    def _():
        prev_a[...] = jnp.zeros((MATS, half, 128), jnp.float32)
        for it in range(ITERS):
            x_in[it] = face_zero

    @pl.when(group == groups - 1)
    def _():
        next_e[...] = jnp.zeros((MATS, half, 128), jnp.float32)
        for it in range(ITERS):
            y_in[it] = face_zero
            g_in[it] = face_zero

    for it in range(ITERS):
        for v in range(NV):
            edge_out[it, 0, v] = state[v, pl.ds(tiles - 1, planes, stride=tiles), :]
            edge_out[it, 1, v] = state[v, pl.ds(0, planes, stride=tiles), :]
        for side in range(2):
            edge_copy(it, side).start()

        def gather(q, carry):
            for k in range(8):
                e = q * 8 + k
                chosen = block_s[e]
                for v in range(NV):
                    gathered[v, pl.ds(e, 1), :] = state[v, pl.ds(chosen, 1), :]
            return carry

        lax.fori_loop(0, senders // 8, gather, 0)
        weight = weight_r[...]
        for v in range(NV):
            chosen = gathered[v]
            moved = chosen
            for bit in range(7):
                rolled = pltpu.roll(moved, 128 - (1 << bit), 1)
                moved = jnp.where((offset_all & (1 << bit)) != 0, rolled, moved)
            placed[:, v * 128:(v + 1) * 128] = split3(weight * (chosen + moved))
        slot_values = jnp.dot(place3, placed[...], preferred_element_type=jnp.float32)
        for v in range(NV):
            for k in range(CAP):
                outgoing[it, pl.ds(v * CAP + k, devices, stride=SLOT_ROWS), :] = slot_values[
                    k * devices:(k + 1) * devices, v * 128:(v + 1) * 128
                ]

        def send(k, carry):
            fringe_copy(it, k).start()
            return carry

        lax.fori_loop(1, devices, send, 0)
        mine = pl.ds(pl.multiple_of(me * SLOT_ROWS, SLOT_ROWS), NV * CAP)
        received[it, mine, :] = outgoing[it, mine, :]

        if it == 0:
            fill_pick()
            for copy in sweep_loads:
                copy.wait()
            lax.fori_loop(0, tiles // 8, transfer, 0)
            for copy in drive_loads:
                copy.wait()
        for side in range(2):
            edge_copy(it, side).wait_recv()
        lane = iota((tiles, 128), 1)
        row = iota((tiles, 128), 0)

        def drive_plane(i, carry):
            rows = pl.ds(pl.multiple_of(i * tiles, tiles), tiles)
            factor = coupling[rows, :]
            for v in range(NV):
                x = state[v, rows, :]
                before = pltpu.roll(edge_in[it, 0, v, pl.ds(i, 1), :], 1, 1)
                after = pltpu.roll(edge_in[it, 1, v, pl.ds(i, 1), :], 127, 1)
                left = pltpu.roll(x, 1, 1)
                left = jnp.where(
                    lane == 0, jnp.where(row == 0, before, pltpu.roll(left, 1, 0)), left
                )
                right = pltpu.roll(x, 127, 1)
                right = jnp.where(
                    lane == 127,
                    jnp.where(row == tiles - 1, after, pltpu.roll(right, tiles - 1, 0)),
                    right,
                )
                drive[v, rows, :] = forcing[v, rows, :] - factor * (2.0 * x - left - right)
            return carry

        lax.fori_loop(0, planes, drive_plane, 0)

        def take(k, carry):
            fringe_copy(it, k).wait_recv()
            return carry

        lax.fori_loop(1, devices, take, 0)
        for v in range(NV):
            parts = [
                received[it, pl.ds(v * CAP + k, devices, stride=SLOT_ROWS), :] for k in range(CAP)
            ]
            stacked[:, v * 128:(v + 1) * 128] = split3(jnp.concatenate(parts, axis=0))

        def add_fringe(i, carry):
            rows = pl.ds(pl.multiple_of(i * tiles, tiles), tiles)
            hole = (1 - blank[rows, :]).astype(jnp.float32)
            fringe = jnp.dot(pick[rows, :], stacked[...], preferred_element_type=jnp.float32)
            for v in range(NV):
                drive[v, rows, :] = drive[v, rows, :] + hole * fringe[:, v * 128:(v + 1) * 128]
            return carry

        lax.fori_loop(0, planes, add_fringe, 0)

        zero_down(it, far_base, 2)
        b_to_partner(it).start()
        zero_down(it, own_base, core)
        zero_up(it, far_base, 2)
        c_to_partner(it).start()
        zero_up(it, own_base, core)

        if it == 0:
            for k in range(3):
                mats_copy(k).wait_recv()
        b_to_partner(it).wait_recv()
        chip_forward(it)

        @pl.when(jnp.logical_not(odd))
        def _():
            b_to_next(it).start()

        if it == 0:
            lax.fori_loop(0, half // 8, compose, 0)

            @pl.when(jnp.logical_not(odd) & (group > 0))
            def _():
                prev_a_copy().start()
                next_e_copy().start()

        c_to_partner(it).wait_recv()
        chip_backward(it)

        @pl.when(odd)
        def _():
            b_to_next(it).wait_recv()

            @pl.when(group > 1)
            def _():
                if it == 0:
                    prev_a_copy().wait_recv()
                x_to_skip(it).wait_recv()

            relay_forward(it)

            @pl.when(group < groups - 1)
            def _():
                x_to_skip(it).start()
                x_to_next(it).start()

        @pl.when(jnp.logical_not(odd))
        def _():
            @pl.when(group > 0)
            def _():
                x_to_next(it).wait_recv()
                x_face[it, 0, :, own_rows, :] = x_in[it]

            @pl.when(group == 0)
            def _():
                x_face[it, 0, :, own_rows, :] = face_zero

        turn(it)

        @pl.when(jnp.logical_not(odd) & (group > 0))
        def _():
            g_to_prev(it).start()

        def pass_back():
            relay_backward(it)
            y_to_prev(it).start()

            @pl.when(group > 1)
            def _():
                y_to_skip(it).start()

        @pl.when(group == groups - 1)
        def _():
            pass_back()

        inner_forward(it)
        x_to_partner(it).start()
        true_down(it, own_base)
        x_to_partner(it).wait_recv()
        true_down(it, far_base)

        @pl.when(odd & (group < groups - 1))
        def _():
            g_to_prev(it).wait_recv()
            if it == 0:
                next_e_copy().wait_recv()
            y_to_skip(it).wait_recv()
            pass_back()

        @pl.when(jnp.logical_not(odd))
        def _():
            y_to_prev(it).wait_recv()
            y_face[it, 1, :, own_rows, :] = y_in[it]

        inner_backward(it)
        y_to_partner(it).start()
        true_up(it, own_base)
        if it == ITERS - 1:
            for copy in out_copies(0, own_base):
                copy.start()
        y_to_partner(it).wait_recv()
        true_up(it, far_base)
        if it == ITERS - 1:
            for copy in out_copies(1, far_base):
                copy.start()

    for k in range(3):
        mats_copy(k).wait_send()

    @pl.when(jnp.logical_not(odd) & (group > 0))
    def _():
        prev_a_copy().wait_send()
        next_e_copy().wait_send()

    for it in range(ITERS):
        for side in range(2):
            edge_copy(it, side).wait_send()

        def sent(k, carry):
            fringe_copy(it, k).wait_send()
            return carry

        lax.fori_loop(1, devices, sent, 0)
        b_to_partner(it).wait_send()
        c_to_partner(it).wait_send()
        x_to_partner(it).wait_send()
        y_to_partner(it).wait_send()

        @pl.when(jnp.logical_not(odd))
        def _():
            b_to_next(it).wait_send()

            @pl.when(group > 0)
            def _():
                g_to_prev(it).wait_send()

        @pl.when(odd)
        def _():
            y_to_prev(it).wait_send()

            @pl.when(group > 1)
            def _():
                y_to_skip(it).wait_send()

            @pl.when(group < groups - 1)
            def _():
                x_to_skip(it).wait_send()
                x_to_next(it).wait_send()

    for part, base in enumerate((own_base, far_base)):
        for copy in out_copies(part, base):
            copy.wait()


def shards(
    initial_state, forcing, block_inverse, lower_decay, upper_decay, cross_coupling, iblank,
    donor_receiver, donor_block, stencil_offset, stencil_weight, fringe_target,
):
    ns, nc = lax.axis_size("stream"), lax.axis_size("cross")
    devices = ns * nc
    planes, cells = initial_state.shape[1:]
    tiles = cells // 128
    senders = donor_block.shape[0]
    slots = devices * CAP

    def tiled(x):
        lead = x.shape[:-2]
        n = len(lead)
        order = tuple(range(n)) + (n + 1, n, n + 2)
        return x.reshape(lead + (planes, tiles, 128)).transpose(order)

    def untiled(x):
        return x.transpose(0, 2, 1, 3).reshape(NV, planes, cells)

    full = (NV, planes * tiles, 128)
    half = tiles // 2
    f32, bf16 = jnp.float32, jnp.bfloat16
    dma = pltpu.SemaphoreType.DMA
    face = pltpu.VMEM((ITERS, NV, half, 128), f32)
    out = jax.ShapeDtypeStruct((NV, tiles, planes, 128), f32)
    hbm = pl.BlockSpec(memory_space=pl.ANY)
    vmem = pl.BlockSpec(memory_space=pltpu.VMEM)
    smem = pl.BlockSpec(memory_space=pltpu.SMEM)
    final, update = pl.pallas_call(
        functools.partial(kernel, ns, nc, planes, tiles),
        out_shape=(out, out),
        in_specs=[hbm] * 7 + [vmem, smem, vmem, vmem, vmem],
        out_specs=(hbm, hbm),
        scratch_shapes=[
            pltpu.VMEM(full, f32),
            pltpu.VMEM(full, f32),
            pltpu.VMEM((len(PAIRS),) + full[1:], f32),
            pltpu.VMEM(full, f32),
            pltpu.VMEM(full, f32),
            pltpu.VMEM(full[1:], f32),
            pltpu.VMEM(full[1:], jnp.int32),
            pltpu.VMEM(full, f32),
            pltpu.VMEM(full, f32),
            pltpu.VMEM(full, f32),
            pltpu.VMEM((NV, senders, 128), f32),
            pltpu.VMEM((3 * senders, NV * 128), bf16),
            pltpu.VMEM((ITERS, devices * SLOT_ROWS, 128), f32),
            pltpu.VMEM((ITERS, devices * SLOT_ROWS, 128), f32),
            pltpu.VMEM((planes * tiles, 3 * slots), bf16),
            pltpu.VMEM((3 * slots, NV * 128), bf16),
            pltpu.VMEM((ITERS, 2, NV, planes, 128), f32),
            pltpu.VMEM((ITERS, 2, NV, planes, 128), f32),
            pltpu.VMEM((planes, MATS, 8, 128), f32),
            pltpu.VMEM((3, 3 * MATS, half, 128), f32),
            pltpu.VMEM((3 * MATS, half, 128), f32),
            pltpu.VMEM((MATS, half, 128), f32),
            pltpu.VMEM((MATS, half, 128), f32),
            pltpu.VMEM((ITERS, 3, 2, NV, half, 128), f32),
            face,
            face,
            face,
            face,
            face,
            pltpu.VMEM((ITERS, 2, NV, tiles, 128), f32),
            face,
            face,
            face,
            face,
            pltpu.VMEM((ITERS, 2, NV, tiles, 128), f32),
            dma((planes * (4 + 2 + NV),)),
            dma((2, planes, 2)),
            dma((ITERS, devices)),
            dma((ITERS, devices)),
            dma((ITERS, 2)),
            dma((ITERS, 2)),
            dma((5,)),
            dma((5,)),
            dma((ITERS, 10)),
            dma((ITERS, 8)),
        ],
        compiler_params=pltpu.CompilerParams(
            collective_id=0, has_side_effects=True, vmem_limit_bytes=56 * 1024 * 1024
        ),
    )(
        tiled(initial_state), tiled(forcing), tiled(block_inverse), tiled(lower_decay),
        tiled(upper_decay), tiled(cross_coupling), tiled(iblank),
        donor_receiver.reshape(1, senders), donor_block, stencil_offset.reshape(1, senders), stencil_weight,
        fringe_target.reshape(1, slots),
    )
    return untiled(final), untiled(update)


def solution(mesh):
    return jax.shard_map(
        shards,
        mesh=mesh,
        in_specs=(
            P(None, "stream", "cross"),
            P(None, "stream", "cross"),
            P(None, None, "stream", "cross"),
            P(None, "stream", "cross"),
            P(None, "stream", "cross"),
            P("stream", "cross"),
            P("stream", "cross"),
            P(("stream", "cross"), None),
            P(("stream", "cross")),
            P(("stream", "cross")),
            P(("stream", "cross"), None),
            P(("stream", "cross")),
        ),
        out_specs=(P(None, "stream", "cross"), P(None, "stream", "cross")),
        check_vma=False,
    )
```

time: 95.3 us -> 89.1 us (0.935)
  Pallas kernels: 90.8 us -> 84.6 us
    pallas_call x1, Pallas kernels: 90.8 us -> 84.6 us  [shards(): pl.pallas_call(functools.partial(kernel, ns, nc, planes, tiles), out_shap...]
where the time goes in v1:
time: 89.1 us; the launch traced here: 88.9 us
  Pallas kernels  84.6 us (95%)
  local copies, waits for them, and re-layouts  3.62 us (4%)
    pallas_call x1, Pallas kernels, shards(): pl.pallas_call(functools.partial(kernel, ns, nc, planes, tiles), out_shap...  84.6 us
    unnamed x4, local copies, waits for them, and re-layouts  3.62 us

profile of v1, /device:TPU:0, one launch (start us, length us, event | category | flops | bytes accessed | tf_op | source)
XLA Modules:
  0.0 88.9 jit_solution(2613763031795829803)
XLA Ops:
  0.6 84.6 %shard_map.131 = (f32[5,64,8,128]{3,2,1,0:T(8,128)}, f32[5,64,8,128]{3,2,1,0:T(8,128)}) custom-call(f32[5,64,8,128]{3,2,1,0:T(8,128)} %bitcast.31, f32[5,64,8,128]{3,2,1,0:T(8,128)} %bitcast.32, f32[5,5,64,8,128]{4,3,2,1,0:T(8,128)} %bitcast.30, f32[5,64,8,128]{3,2,1,0:T(8,128)} %bitcast.33, f32[5,64,8,128]{3,2,1,0:T(8,128)} %bitcast.34, ...), custom_call_target="tpu_custom_call" | custom-call | tf_op jit(solution)/shard_map/pallas_call | solution.py:767
  85.2 0.0 copy-start
  85.2 2.6 %copy.16 = f32[5,8,8192]{2,1,0:T(8,128)} copy(f32[5,8,8192]{2,1,0:T(8,128)} %bitcast.36) | data formatting | bytes 2621440
  87.8 0.0 copy-done
  87.8 1.1 %copy.17 = f32[5,8,8192]{2,1,0:T(8,128)} copy(f32[5,8,8192]{2,1,0:T(8,128)S(1)} %bitcast.35) | data formatting | bytes 2621440
Async XLA Ops:
  85.2 2.6 %copy-start = (f32[5,64,8,128]{3,2,1,0:T(8,128)S(1)}, f32[5,64,8,128]{3,2,1,0:T(8,128)}, u32[]{:S(2)}) copy-start(f32[5,64,8,128]{3,2,1,0:T(8,128)} %get-tuple-element.5) | copy-start | bytes 3932164

commit v2 on v1

--- a/solution.py
+++ b/solution.py
@@ -12,7 +12,9 @@
 NV = 5
 SLOT_ROWS = 16
 STEP = 16
+PART = 8
 MATS = NV * NV
+BATCHES = ((0, 1, 2, 3, 4),)
 MESH = pl.DeviceIdType.MESH
 PAIRS = [(a, b) for a in range(NV) for b in range(a, NV)]
 
@@ -41,8 +43,8 @@
     state, forcing, inverse, lower, upper, coupling, blank,
     drive, near, update, gathered, placed, outgoing, received, pick, stacked,
     edge_out, edge_in,
-    stage, mats, comp, prev_a, next_e,
-    zero, chip_b, chip_c, prev_b, x_in, x_out, x_face, g_own, g_in, y_in, y_out, y_face,
+    stage, mats, comp,
+    zero, chip_b, chip_c, x_in, x_out, x_face, g_own, g_inner, y_in, y_out, y_face,
     load_sem, out_sem, fsend, frecv, esend, erecv, msend, mrecv, csend, crecv,
 ):
     s, c = lax.axis_index("stream"), lax.axis_index("cross")
@@ -54,7 +56,7 @@
     half = tiles // 2
     core = lax.rem(s, 2)
     group = s // 2
-    odd = lax.rem(group, 2) == 1
+    first, last = group == 0, group == groups - 1
     own_base = lax.rem(core + group, 2) * half
     far_base = half - own_base
 
@@ -69,36 +71,36 @@
     def rows_of(i):
         return pl.ds(i * tiles, tiles)
 
-    state_loads = [load(state_h.at[:, :, i, :], state.at[:, rows_of(i), :]) for i in range(planes)]
     sweep_loads = []
     for i in range(planes):
         sweep_loads.append(load(lower_h.at[:, :, i, :], lower.at[:, rows_of(i), :]))
         for a in range(NV):
-            first = pair(a, a)
+            top = pair(a, a)
             sweep_loads.append(
                 load(
                     inverse_h.at[a, pl.ds(a, NV - a), :, i, :],
-                    inverse.at[pl.ds(first, NV - a), rows_of(i), :],
+                    inverse.at[pl.ds(top, NV - a), rows_of(i), :],
                 )
             )
     for i in range(planes):
         sweep_loads.append(load(upper_h.at[:, :, i, :], upper.at[:, rows_of(i), :]))
+    barrier = pltpu.get_barrier_semaphore()
+
+    def greet(k, carry):
+        other = lax.rem(me + k, devices)
+        pl.semaphore_signal(
+            barrier, inc=1, device_id=(other // nc, lax.rem(other, nc)), device_id_type=MESH
+        )
+        return carry
+
+    lax.fori_loop(1, devices, greet, 0)
+
+    state_loads = [load(state_h.at[:, :, i, :], state.at[:, rows_of(i), :]) for i in range(planes)]
     drive_loads = []
     for i in range(planes):
         drive_loads.append(load(forcing_h.at[:, :, i, :], forcing.at[:, rows_of(i), :]))
         drive_loads.append(load(coupling_h.at[:, i, :], coupling.at[rows_of(i), :]))
         drive_loads.append(load(blank_h.at[:, i, :], blank.at[rows_of(i), :]))
-
-    barrier = pltpu.get_barrier_semaphore()
-
-    def greet(k, carry):
-        other = lax.rem(me + k, devices)
-        pl.semaphore_signal(
-            barrier, inc=1, device_id=(other // nc, lax.rem(other, nc)), device_id_type=MESH
-        )
-        return carry
-
-    lax.fori_loop(1, devices, greet, 0)
 
     eye = iota((senders, senders), 0) == iota((senders, senders), 1)
     recv_row = receiver_r[...].astype(jnp.float32)
@@ -136,10 +138,6 @@
 
         lax.fori_loop(0, planes, fill, 0)
 
-    for copy in state_loads:
-        copy.wait()
-    pl.semaphore_wait(barrier, devices - 1)
-
     def fringe_copy(it, k):
         other = lax.rem(me + k, devices)
         start = pl.multiple_of(other * SLOT_ROWS, SLOT_ROWS)
@@ -190,59 +188,40 @@
             device_id_type=MESH,
         )
 
-    def prev_a_copy():
-        return pltpu.make_async_remote_copy(
-            src_ref=comp.at[pl.ds(0, MATS)],
-            dst_ref=prev_a,
-            send_sem=msend.at[3],
-            recv_sem=mrecv.at[3],
-            device_id=(member(group + 1, True), c),
-            device_id_type=MESH,
-        )
-
-    def next_e_copy():
-        return pltpu.make_async_remote_copy(
-            src_ref=comp.at[pl.ds(MATS, MATS)],
-            dst_ref=next_e,
-            send_sem=msend.at[4],
-            recv_sem=mrecv.at[4],
-            device_id=(member(group - 1, True), c),
-            device_id_type=MESH,
-        )
-
     def b_to_partner(it):
         return face_copy(it, 0, 0, zero.at[it, 2, 0], zero.at[it, core, 0], partner)
 
     def c_to_partner(it):
         return face_copy(it, 1, 1, zero.at[it, 2, 1], zero.at[it, core, 1], partner)
 
-    def b_to_next(it):
-        return face_copy(it, 2, 2, chip_b.at[it], prev_b.at[it], member(group + 1, True))
-
-    def x_to_next(it):
-        return face_copy(it, 3, 3, x_out.at[it], x_in.at[it], member(group + 1, True))
-
-    def x_to_skip(it):
-        return face_copy(it, 3, 4, x_out.at[it], x_in.at[it], member(group + 2, False))
-
-    def g_to_prev(it):
-        return face_copy(it, 4, 5, g_own.at[it], g_in.at[it], member(group - 1, True))
-
-    def y_to_prev(it):
-        return face_copy(it, 5, 6, y_out.at[it], y_in.at[it], member(group - 1, True))
-
-    def y_to_skip(it):
-        return face_copy(it, 5, 7, y_out.at[it], y_in.at[it], member(group - 2, False))
+    parts = [pl.ds(k * PART, PART) for k in range(half // PART)]
+
+    def x_to_next(it, k, source):
+        rows = parts[k]
+        return face_copy(
+            it, 2 + k, 2 + k, source.at[it, :, rows, :], x_in.at[it, :, rows, :], member(group + 1, True)
+        )
+
+    def y_to_prev(it, k):
+        rows = parts[k]
+        n = 2 + len(parts) + k
+        return face_copy(
+            it, n, n, y_out.at[it, :, rows, :], y_in.at[it, :, rows, :], member(group - 1, True)
+        )
 
     own_rows = pl.ds(pl.multiple_of(own_base, half), half)
 
     def x_to_partner(it):
         source = x_face.at[it, 1 - core, :, own_rows, :]
-        return face_copy(it, 6, 8, source, source, partner)
-
-    def y_to_partner(it):
-        source = y_face.at[it, 1 - core, :, own_rows, :]
-        return face_copy(it, 7, 9, source, source, partner)
+        n = 2 + 2 * len(parts)
+        return face_copy(it, n, n, source, source, partner)
+
+    def y_to_partner(it, k, send):
+        side, base = (1 - core, own_base) if send else (core, far_base)
+        rows = pl.ds(pl.multiple_of(base + k * PART, PART), PART)
+        source = y_face.at[it, side, :, rows, :]
+        n = 3 + 2 * len(parts) + k
+        return face_copy(it, n, n, source, source, partner)
 
     def block(rows):
         return [inverse[k, rows, :] for k in range(len(PAIRS))]
@@ -267,6 +246,45 @@
 
     def column(m, b):
         return [m[a][b] for a in range(NV)]
+
+    def send_donors(it):
+        for v in range(NV):
+            edge_out[it, 0, v] = state[v, pl.ds(tiles - 1, planes, stride=tiles), :]
+            edge_out[it, 1, v] = state[v, pl.ds(0, planes, stride=tiles), :]
+        for side in range(2):
+            edge_copy(it, side).start()
+
+        def gather(q, carry):
+            for k in range(8):
+                e = q * 8 + k
+                chosen = block_s[e]
+                for v in range(NV):
+                    gathered[v, pl.ds(e, 1), :] = state[v, pl.ds(chosen, 1), :]
+            return carry
+
+        lax.fori_loop(0, senders // 8, gather, 0)
+        weight = weight_r[...]
+        for v in range(NV):
+            chosen = gathered[v]
+            moved = chosen
+            for bit in range(7):
+                rolled = pltpu.roll(moved, 128 - (1 << bit), 1)
+                moved = jnp.where((offset_all & (1 << bit)) != 0, rolled, moved)
+            placed[:, v * 128:(v + 1) * 128] = split3(weight * (chosen + moved))
+        slot_values = jnp.dot(place3, placed[...], preferred_element_type=jnp.float32)
+        for v in range(NV):
+            for k in range(CAP):
+                outgoing[it, pl.ds(v * CAP + k, devices, stride=SLOT_ROWS), :] = slot_values[
+                    k * devices:(k + 1) * devices, v * 128:(v + 1) * 128
+                ]
+
+        def send(k, carry):
+            fringe_copy(it, k).start()
+            return carry
+
+        lax.fori_loop(1, devices, send, 0)
+        mine = pl.ds(pl.multiple_of(me * SLOT_ROWS, SLOT_ROWS), NV * CAP)
+        received[it, mine, :] = outgoing[it, mine, :]
 
     def transfer(q, carry):
         each = half // 8
@@ -274,52 +292,63 @@
         base = jnp.where(q < each, far_base, own_base) + local
         slot = jnp.where(q < each, 2, core)
         spot = at(local, 8)
-        chain = None
-        for i in range(planes):
-            rows = at(i * tiles + base, 8)
-            blocks = block(rows)
-            factor = [lower[v, rows, :] for v in range(NV)]
-            if i == 0:
-                chain = [[blocks[pair(a, b)] * factor[b] for a in range(NV)] for b in range(NV)]
-            else:
-                chain = [
-                    apply(blocks, [factor[v] * chain[b][v] for v in range(NV)]) for b in range(NV)
-                ]
-            for b in range(NV):
+        for cols in BATCHES:
+            chain = None
+            for i in range(planes):
+                rows = at(i * tiles + base, 8)
+                blocks = block(rows)
+                factor = [lower[v, rows, :] for v in range(NV)]
+                if i == 0:
+                    chain = {b: [blocks[pair(a, b)] * factor[b] for a in range(NV)] for b in cols}
+                else:
+                    chain = {
+                        b: apply(blocks, [factor[v] * chain[b][v] for v in range(NV)]) for b in cols
+                    }
+                if i < planes - 1:
+                    for b in cols:
+                        for a in range(NV):
+                            stage[i, a * NV + b] = chain[b][a]
+            for b in cols:
                 for a in range(NV):
-                    stage[i, a * NV + b] = chain[b][a]
-        for b in range(NV):
-            for a in range(NV):
-                mats[slot, a * NV + b, spot, :] = chain[b][a]
-        both = chain
-        for i in reversed(range(planes - 1)):
-            rows = at(i * tiles + base, 8)
-            blocks = block(rows)
-            factor = [upper[v, rows, :] for v in range(NV)]
-            both = [
-                [
-                    stage[i, a * NV + b] + z
-                    for a, z in enumerate(apply(blocks, [factor[v] * both[b][v] for v in range(NV)]))
-                ]
-                for b in range(NV)
-            ]
-        for b in range(NV):
-            for a in range(NV):
-                mats[slot, 2 * MATS + a * NV + b, spot, :] = both[b][a]
-        back = None
-        for i in reversed(range(planes)):
-            rows = at(i * tiles + base, 8)
-            blocks = block(rows)
-            factor = [upper[v, rows, :] for v in range(NV)]
-            if i == planes - 1:
-                back = [[blocks[pair(a, b)] * factor[b] for a in range(NV)] for b in range(NV)]
-            else:
-                back = [
-                    apply(blocks, [factor[v] * back[b][v] for v in range(NV)]) for b in range(NV)
-                ]
-        for b in range(NV):
-            for a in range(NV):
-                mats[slot, MATS + a * NV + b, spot, :] = back[b][a]
+                    mats[slot, a * NV + b, spot, :] = chain[b][a]
+            both = chain
+            for i in reversed(range(planes - 1)):
+                rows = at(i * tiles + base, 8)
+                blocks = block(rows)
+                factor = [upper[v, rows, :] for v in range(NV)]
+                both = {
+                    b: [
+                        stage[i, a * NV + b] + z
+                        for a, z in enumerate(
+                            apply(blocks, [factor[v] * both[b][v] for v in range(NV)])
+                        )
+                    ]
+                    for b in cols
+                }
+            for b in cols:
+                for a in range(NV):
+                    mats[slot, 2 * MATS + a * NV + b, spot, :] = both[b][a]
+            back = None
+            for i in reversed(range(planes)):
+                rows = at(i * tiles + base, 8)
+                blocks = block(rows)
+                factor = [upper[v, rows, :] for v in range(NV)]
+                if i == planes - 1:
+                    back = {b: [blocks[pair(a, b)] * factor[b] for a in range(NV)] for b in cols}
+                else:
+                    back = {
+                        b: apply(blocks, [factor[v] * back[b][v] for v in range(NV)]) for b in cols
+                    }
+            for b in cols:
+                for a in range(NV):
+                    mats[slot, MATS + a * NV + b, spot, :] = back[b][a]
+
+        @pl.when(q == each - 2)
+        def _():
+            for copy in state_loads:
+                copy.wait()
+            pl.semaphore_wait(barrier, devices - 1)
+            send_donors(0)
 
         @pl.when(q == each - 1)
         def _():
@@ -433,13 +462,20 @@
         return at(own_base + g * STEP, STEP)
 
     def relay_forward(it):
-        for g, rows in enumerate(steps):
-            out = times(matrix(prev_a, 0, rows), [x_in[it, v, rows, :] for v in range(NV)])
-            x = [prev_b[it, v, rows, :] + out[v] for v in range(NV)]
+        for k, rows in enumerate(parts):
+            @pl.when(jnp.logical_not(first))
+            def _():
+                x_to_next(it, k, x_out).wait_recv()
+
+            x = [x_in[it, v, rows, :] for v in range(NV)]
             out = times(matrix(comp, 0, rows), x)
             for v in range(NV):
                 x_out[it, v, rows, :] = chip_b[it, v, rows, :] + out[v]
-                x_face[it, 0, v, own(g), :] = x[v]
+                x_face[it, 0, v, at(own_base + k * PART, PART), :] = x[v]
+
+            @pl.when(jnp.logical_not(first | last))
+            def _():
+                x_to_next(it, k, x_out).start()
 
     def turn(it):
         for g, rows in enumerate(steps):
@@ -452,81 +488,49 @@
         for g, rows in enumerate(steps):
             x = [x_face[it, 0, v, own(g), :] for v in range(NV)]
             out = times(matrix(mats.at[0], 0, rows), x)
-            for v in range(NV):
-                x_face[it, 1, v, own(g), :] = zero[it, 0, 0, v, rows, :] + out[v]
+            high = [zero[it, 0, 0, v, rows, :] + out[v] for v in range(NV)]
+            out = times(matrix(mats.at[1], 2 * MATS, rows), high)
+            for v in range(NV):
+                x_face[it, 1, v, own(g), :] = high[v]
+                g_inner[it, v, rows, :] = zero[it, 1, 1, v, rows, :] + out[v]
 
     def relay_backward(it):
-        for g, rows in enumerate(steps):
-            out = times(matrix(next_e, 0, rows), [y_in[it, v, rows, :] for v in range(NV)])
-            y = [g_in[it, v, rows, :] + out[v] for v in range(NV)]
+        for k, rows in enumerate(parts):
+            @pl.when(jnp.logical_not(last))
+            def _():
+                y_to_prev(it, k).wait_recv()
+
+            y = [y_in[it, v, rows, :] for v in range(NV)]
             out = times(matrix(comp, MATS, rows), y)
             for v in range(NV):
                 y_out[it, v, rows, :] = g_own[it, v, rows, :] + out[v]
-                y_face[it, 1, v, own(g), :] = y[v]
-
-    def inner_backward(it):
-        for g, rows in enumerate(steps):
-            x = [x_face[it, 1, v, own(g), :] for v in range(NV)]
-            out = times(matrix(mats.at[1], 2 * MATS, rows), x)
-            y = [y_face[it, 1, v, own(g), :] for v in range(NV)]
+
+            @pl.when(jnp.logical_not(first))
+            def _():
+                y_to_prev(it, k).start()
+
+            mine = at(own_base + k * PART, PART)
             back = times(matrix(mats.at[1], MATS, rows), y)
             for v in range(NV):
-                y_face[it, 0, v, own(g), :] = zero[it, 1, 1, v, rows, :] + out[v] + back[v]
+                y_face[it, 1, v, mine, :] = y[v]
+                y_face[it, 0, v, mine, :] = g_inner[it, v, rows, :] + back[v]
+            y_to_partner(it, k, True).start()
 
     face_zero = jnp.zeros((NV, half, 128), jnp.float32)
 
-    @pl.when(group == 1)
+    @pl.when(first)
     def _():
-        prev_a[...] = jnp.zeros((MATS, half, 128), jnp.float32)
         for it in range(ITERS):
             x_in[it] = face_zero
 
-    @pl.when(group == groups - 1)
+    @pl.when(last)
     def _():
-        next_e[...] = jnp.zeros((MATS, half, 128), jnp.float32)
         for it in range(ITERS):
             y_in[it] = face_zero
-            g_in[it] = face_zero
 
     for it in range(ITERS):
-        for v in range(NV):
-            edge_out[it, 0, v] = state[v, pl.ds(tiles - 1, planes, stride=tiles), :]
-            edge_out[it, 1, v] = state[v, pl.ds(0, planes, stride=tiles), :]
-        for side in range(2):
-            edge_copy(it, side).start()
-
-        def gather(q, carry):
-            for k in range(8):
-                e = q * 8 + k
-                chosen = block_s[e]
-                for v in range(NV):
-                    gathered[v, pl.ds(e, 1), :] = state[v, pl.ds(chosen, 1), :]
-            return carry
-
-        lax.fori_loop(0, senders // 8, gather, 0)
-        weight = weight_r[...]
-        for v in range(NV):
-            chosen = gathered[v]
-            moved = chosen
-            for bit in range(7):
-                rolled = pltpu.roll(moved, 128 - (1 << bit), 1)
-                moved = jnp.where((offset_all & (1 << bit)) != 0, rolled, moved)
-            placed[:, v * 128:(v + 1) * 128] = split3(weight * (chosen + moved))
-        slot_values = jnp.dot(place3, placed[...], preferred_element_type=jnp.float32)
-        for v in range(NV):
-            for k in range(CAP):
-                outgoing[it, pl.ds(v * CAP + k, devices, stride=SLOT_ROWS), :] = slot_values[
-                    k * devices:(k + 1) * devices, v * 128:(v + 1) * 128
-                ]
-
-        def send(k, carry):
-            fringe_copy(it, k).start()
-            return carry
-
-        lax.fori_loop(1, devices, send, 0)
-        mine = pl.ds(pl.multiple_of(me * SLOT_ROWS, SLOT_ROWS), NV * CAP)
-        received[it, mine, :] = outgoing[it, mine, :]
-
+        if it > 0:
+            send_donors(it)
         if it == 0:
             fill_pick()
             for copy in sweep_loads:
@@ -534,8 +538,6 @@
             lax.fori_loop(0, tiles // 8, transfer, 0)
             for copy in drive_loads:
                 copy.wait()
-        for side in range(2):
-            edge_copy(it, side).wait_recv()
         lane = iota((tiles, 128), 1)
         row = iota((tiles, 128), 0)
 
@@ -544,22 +546,29 @@
             factor = coupling[rows, :]
             for v in range(NV):
                 x = state[v, rows, :]
-                before = pltpu.roll(edge_in[it, 0, v, pl.ds(i, 1), :], 1, 1)
-                after = pltpu.roll(edge_in[it, 1, v, pl.ds(i, 1), :], 127, 1)
                 left = pltpu.roll(x, 1, 1)
                 left = jnp.where(
-                    lane == 0, jnp.where(row == 0, before, pltpu.roll(left, 1, 0)), left
+                    lane == 0, jnp.where(row == 0, 0.0, pltpu.roll(left, 1, 0)), left
                 )
                 right = pltpu.roll(x, 127, 1)
                 right = jnp.where(
                     lane == 127,
-                    jnp.where(row == tiles - 1, after, pltpu.roll(right, tiles - 1, 0)),
+                    jnp.where(row == tiles - 1, 0.0, pltpu.roll(right, tiles - 1, 0)),
                     right,
                 )
                 drive[v, rows, :] = forcing[v, rows, :] - factor * (2.0 * x - left - right)
             return carry
 
         lax.fori_loop(0, planes, drive_plane, 0)
+        for side in range(2):
+            edge_copy(it, side).wait_recv()
+            rows = pl.ds(0 if side == 0 else tiles - 1, planes, stride=tiles)
+            hit = iota((planes, 128), 1) == (0 if side == 0 else 127)
+            for v in range(NV):
+                beyond = pltpu.roll(edge_in[it, side, v], 1 if side == 0 else 127, 1)
+                drive[v, rows, :] = drive[v, rows, :] + coupling[rows, :] * jnp.where(
+                    hit, beyond, 0.0
+                )
 
         def take(k, carry):
             fringe_copy(it, k).wait_recv()
@@ -567,10 +576,10 @@
 
         lax.fori_loop(1, devices, take, 0)
         for v in range(NV):
-            parts = [
+            pieces = [
                 received[it, pl.ds(v * CAP + k, devices, stride=SLOT_ROWS), :] for k in range(CAP)
             ]
-            stacked[:, v * 128:(v + 1) * 128] = split3(jnp.concatenate(parts, axis=0))
+            stacked[:, v * 128:(v + 1) * 128] = split3(jnp.concatenate(pieces, axis=0))
 
         def add_fringe(i, carry):
             rows = pl.ds(pl.multiple_of(i * tiles, tiles), tiles)
@@ -580,108 +589,52 @@
                 drive[v, rows, :] = drive[v, rows, :] + hole * fringe[:, v * 128:(v + 1) * 128]
             return carry
 
-        lax.fori_loop(0, planes, add_fringe, 0)
+        lax.fori_loop(0, planes, add_fringe, 0, unroll=True)
 
         zero_down(it, far_base, 2)
         b_to_partner(it).start()
         zero_down(it, own_base, core)
-        zero_up(it, far_base, 2)
-        c_to_partner(it).start()
-        zero_up(it, own_base, core)
-
         if it == 0:
             for k in range(3):
                 mats_copy(k).wait_recv()
         b_to_partner(it).wait_recv()
         chip_forward(it)
 
-        @pl.when(jnp.logical_not(odd))
+        @pl.when(first)
         def _():
-            b_to_next(it).start()
-
+            for k in range(len(parts)):
+                x_to_next(it, k, chip_b).start()
+
+        zero_up(it, far_base, 2)
+        c_to_partner(it).start()
+        zero_up(it, own_base, core)
         if it == 0:
             lax.fori_loop(0, half // 8, compose, 0)
-
-            @pl.when(jnp.logical_not(odd) & (group > 0))
-            def _():
-                prev_a_copy().start()
-                next_e_copy().start()
-
         c_to_partner(it).wait_recv()
         chip_backward(it)
-
-        @pl.when(odd)
+        relay_forward(it)
+        turn(it)
+        inner_forward(it)
+
+        @pl.when(last)
         def _():
-            b_to_next(it).wait_recv()
-
-            @pl.when(group > 1)
-            def _():
-                if it == 0:
-                    prev_a_copy().wait_recv()
-                x_to_skip(it).wait_recv()
-
-            relay_forward(it)
-
-            @pl.when(group < groups - 1)
-            def _():
-                x_to_skip(it).start()
-                x_to_next(it).start()
-
-        @pl.when(jnp.logical_not(odd))
-        def _():
-            @pl.when(group > 0)
-            def _():
-                x_to_next(it).wait_recv()
-                x_face[it, 0, :, own_rows, :] = x_in[it]
-
-            @pl.when(group == 0)
-            def _():
-                x_face[it, 0, :, own_rows, :] = face_zero
-
-        turn(it)
-
-        @pl.when(jnp.logical_not(odd) & (group > 0))
-        def _():
-            g_to_prev(it).start()
-
-        def pass_back():
             relay_backward(it)
-            y_to_prev(it).start()
-
-            @pl.when(group > 1)
-            def _():
-                y_to_skip(it).start()
-
-        @pl.when(group == groups - 1)
-        def _():
-            pass_back()
-
-        inner_forward(it)
+
         x_to_partner(it).start()
         true_down(it, own_base)
         x_to_partner(it).wait_recv()
         true_down(it, far_base)
 
-        @pl.when(odd & (group < groups - 1))
+        @pl.when(jnp.logical_not(last))
         def _():
-            g_to_prev(it).wait_recv()
-            if it == 0:
-                next_e_copy().wait_recv()
-            y_to_skip(it).wait_recv()
-            pass_back()
-
-        @pl.when(jnp.logical_not(odd))
-        def _():
-            y_to_prev(it).wait_recv()
-            y_face[it, 1, :, own_rows, :] = y_in[it]
-
-        inner_backward(it)
-        y_to_partner(it).start()
+            relay_backward(it)
+
         true_up(it, own_base)
         if it == ITERS - 1:
             for copy in out_copies(0, own_base):
                 copy.start()
-        y_to_partner(it).wait_recv()
+        for k in range(len(parts)):
+            y_to_partner(it, k, False).wait_recv()
         true_up(it, far_base)
         if it == ITERS - 1:
             for copy in out_copies(1, far_base):
@@ -690,11 +643,6 @@
     for k in range(3):
         mats_copy(k).wait_send()
 
-    @pl.when(jnp.logical_not(odd) & (group > 0))
-    def _():
-        prev_a_copy().wait_send()
-        next_e_copy().wait_send()
-
     for it in range(ITERS):
         for side in range(2):
             edge_copy(it, side).wait_send()
@@ -707,28 +655,18 @@
         b_to_partner(it).wait_send()
         c_to_partner(it).wait_send()
         x_to_partner(it).wait_send()
-        y_to_partner(it).wait_send()
-
-        @pl.when(jnp.logical_not(odd))
+        for k in range(len(parts)):
+            y_to_partner(it, k, True).wait_send()
+
+        @pl.when(jnp.logical_not(last))
         def _():
-            b_to_next(it).wait_send()
-
-            @pl.when(group > 0)
-            def _():
-                g_to_prev(it).wait_send()
-
-        @pl.when(odd)
+            for k in range(len(parts)):
+                x_to_next(it, k, x_out).wait_send()
+
+        @pl.when(jnp.logical_not(first))
         def _():
-            y_to_prev(it).wait_send()
-
-            @pl.when(group > 1)
-            def _():
-                y_to_skip(it).wait_send()
-
-            @pl.when(group < groups - 1)
-            def _():
-                x_to_skip(it).wait_send()
-                x_to_next(it).wait_send()
+            for k in range(len(parts)):
+                y_to_prev(it, k).wait_send()
 
     for part, base in enumerate((own_base, far_base)):
         for copy in out_copies(part, base):
@@ -791,10 +729,7 @@
             pltpu.VMEM((planes, MATS, 8, 128), f32),
             pltpu.VMEM((3, 3 * MATS, half, 128), f32),
             pltpu.VMEM((3 * MATS, half, 128), f32),
-            pltpu.VMEM((MATS, half, 128), f32),
-            pltpu.VMEM((MATS, half, 128), f32),
             pltpu.VMEM((ITERS, 3, 2, NV, half, 128), f32),
-            face,
             face,
             face,
             face,
@@ -811,10 +746,10 @@
             dma((ITERS, devices)),
             dma((ITERS, 2)),
             dma((ITERS, 2)),
-            dma((5,)),
-            dma((5,)),
-            dma((ITERS, 10)),
-            dma((ITERS, 8)),
+            dma((3,)),
+            dma((3,)),
+            dma((ITERS, 3 + 3 * (half // PART))),
+            dma((ITERS, 3 + 3 * (half // PART))),
         ],
         compiler_params=pltpu.CompilerParams(
             collective_id=0, has_side_effects=True, vmem_limit_bytes=56 * 1024 * 1024

time: 89.1 us -> 78.4 us (0.88)
  Pallas kernels: 84.6 us -> 73.9 us
    pallas_call x1, Pallas kernels: 84.6 us -> 73.9 us  [shards(): pl.pallas_call(functools.partial(kernel, ns, nc, planes, tiles), out_shap...]
where the time goes in v2:
time: 78.4 us; the launch traced here: 78.2 us
  Pallas kernels  73.9 us (94%)
  local copies, waits for them, and re-layouts  3.62 us (5%)
    pallas_call x1, Pallas kernels, shards(): pl.pallas_call(functools.partial(kernel, ns, nc, planes, tiles), out_shap...  73.9 us
    unnamed x4, local copies, waits for them, and re-layouts  3.62 us

profile of v2, /device:TPU:0, one launch (start us, length us, event | category | flops | bytes accessed | tf_op | source)
XLA Modules:
  0.0 78.2 jit_solution(4417601730438386464)
XLA Ops:
  0.6 73.9 %shard_map.131 = (f32[5,64,8,128]{3,2,1,0:T(8,128)}, f32[5,64,8,128]{3,2,1,0:T(8,128)}) custom-call(f32[5,64,8,128]{3,2,1,0:T(8,128)} %bitcast.31, f32[5,64,8,128]{3,2,1,0:T(8,128)} %bitcast.32, f32[5,5,64,8,128]{4,3,2,1,0:T(8,128)} %bitcast.30, f32[5,64,8,128]{3,2,1,0:T(8,128)} %bitcast.33, f32[5,64,8,128]{3,2,1,0:T(8,128)} %bitcast.34, ...), custom_call_target="tpu_custom_call" | custom-call | tf_op jit(solution)/shard_map/pallas_call | solution.py:705
  74.5 0.0 copy-start
  74.5 2.6 %copy.16 = f32[5,8,8192]{2,1,0:T(8,128)} copy(f32[5,8,8192]{2,1,0:T(8,128)} %bitcast.36) | data formatting | bytes 2621440
  77.1 0.0 copy-done
  77.1 1.1 %copy.17 = f32[5,8,8192]{2,1,0:T(8,128)} copy(f32[5,8,8192]{2,1,0:T(8,128)S(1)} %bitcast.35) | data formatting | bytes 2621440
Async XLA Ops:
  74.5 2.6 %copy-start = (f32[5,64,8,128]{3,2,1,0:T(8,128)S(1)}, f32[5,64,8,128]{3,2,1,0:T(8,128)}, u32[]{:S(2)}) copy-start(f32[5,64,8,128]{3,2,1,0:T(8,128)} %get-tuple-element.5) | copy-start | bytes 3932164

commit v3 on v2

--- a/solution.py
+++ b/solution.py
@@ -14,6 +14,7 @@
 STEP = 16
 PART = 8
 MATS = NV * NV
+PIECES = ((0, 13), (13, 12))
 BATCHES = ((0, 1, 2, 3, 4),)
 MESH = pl.DeviceIdType.MESH
 PAIRS = [(a, b) for a in range(NV) for b in range(a, NV)]
@@ -43,9 +44,10 @@
     state, forcing, inverse, lower, upper, coupling, blank,
     drive, near, update, gathered, placed, outgoing, received, pick, stacked,
     edge_out, edge_in,
-    stage, mats, comp,
+    stage, mats, comp, all_m, all_b, all_g,
     zero, chip_b, chip_c, x_in, x_out, x_face, g_own, g_inner, y_in, y_out, y_face,
     load_sem, out_sem, fsend, frecv, esend, erecv, msend, mrecv, csend, crecv,
+    asend, arecv, dsend, drecv,
 ):
     s, c = lax.axis_index("stream"), lax.axis_index("cross")
     devices = ns * nc
@@ -57,6 +59,7 @@
     core = lax.rem(s, 2)
     group = s // 2
     first, last = group == 0, group == groups - 1
+    even = lax.rem(group, 2) == 0
     own_base = lax.rem(core + group, 2) * half
     far_base = half - own_base
 
@@ -187,6 +190,93 @@
             device_id=(partner, c),
             device_id_type=MESH,
         )
+
+    def chip_copy(kind, piece, sender, d):
+        first_row, size = piece
+        away = d if kind == 0 else -d
+        return pltpu.make_async_remote_copy(
+            src_ref=comp.at[pl.ds(kind * MATS + first_row, size)],
+            dst_ref=all_m.at[kind, sender, pl.ds(first_row, size)],
+            send_sem=asend.at[kind, PIECES.index(piece), d],
+            recv_sem=arecv.at[kind, PIECES.index(piece), sender],
+            device_id=(member(group + away, d % 2 == 1), c),
+            device_id_type=MESH,
+        )
+
+    def chip_to(kind, d):
+        inside = (group > 0) & (group < groups - 1)
+        return inside & ((group + d < groups) if kind == 0 else (group >= d))
+
+    def pass_copy(kind, piece, owner):
+        rows = pl.ds(piece[0], piece[1])
+        source = all_m.at[kind, owner, rows]
+        return pltpu.make_async_remote_copy(
+            src_ref=source,
+            dst_ref=source,
+            send_sem=asend.at[kind, PIECES.index(piece), 0],
+            recv_sem=arecv.at[kind, PIECES.index(piece), owner],
+            device_id=(member(group + (1 if kind else -1), True), c),
+            device_id_type=MESH,
+        )
+
+    def passes(kind):
+        return (even & (group < groups - 2)) if kind else (jnp.logical_not(even) & (group > 1))
+
+    def wait_chip(kind, owner):
+        for piece in PIECES:
+            chip_copy(kind, piece, owner, 1).wait_recv()
+
+    def wait_mats(kind):
+        end = first if kind else last
+        for i in range(1, groups - 1):
+            due = (group < i) if kind else (group > i)
+            passed = passes(kind) & (group == (i - 2 if kind else i + 2)) & jnp.logical_not(end)
+
+            @pl.when(due & jnp.logical_not(passed))
+            def _():
+                wait_chip(kind, i)
+
+    def pass_on(kind):
+        end = first if kind else last
+        owner = group + (2 if kind else -2)
+
+        @pl.when(passes(kind))
+        def _():
+            @pl.when(jnp.logical_not(end))
+            def _():
+                wait_chip(kind, owner)
+
+            for piece in PIECES:
+                pass_copy(kind, piece, owner).start()
+
+    def send_chip(kind, d, pieces, extra):
+        @pl.when(chip_to(kind, d) & extra)
+        def _():
+            for piece in pieces:
+                chip_copy(kind, piece, group, d).start()
+
+    def direct_copy(it, kind, sender, d):
+        source, target = ((chip_b, all_b), (g_own, all_g))[kind]
+        away = d if kind == 0 else -d
+        return pltpu.make_async_remote_copy(
+            src_ref=source.at[it],
+            dst_ref=target.at[it, sender],
+            send_sem=dsend.at[it, kind, d],
+            recv_sem=drecv.at[it, kind, sender],
+            device_id=(member(group + away, d % 2 == 1), c),
+            device_id_type=MESH,
+        )
+
+    def direct_to(it, kind, d):
+        if it == 0:
+            return (group + d == groups - 1) if kind == 0 else (group == d)
+        return (group + d < groups) if kind == 0 else (group >= d)
+
+    def send_direct(it, kind):
+        for d in reversed(range(1, groups)):
+            @pl.when(direct_to(it, kind, d))
+            def _():
+                direct_copy(it, kind, group, d).start()
 
     def b_to_partner(it):
         return face_copy(it, 0, 0, zero.at[it, 2, 0], zero.at[it, core, 0], partner)
@@ -473,7 +563,7 @@
                 x_out[it, v, rows, :] = chip_b[it, v, rows, :] + out[v]
                 x_face[it, 0, v, at(own_base + k * PART, PART), :] = x[v]
 
-            @pl.when(jnp.logical_not(first | last))
+            @pl.when((group > 0) & (group < groups - 2))
             def _():
                 x_to_next(it, k, x_out).start()
 
@@ -505,7 +595,7 @@
             for v in range(NV):
                 y_out[it, v, rows, :] = g_own[it, v, rows, :] + out[v]
 
-            @pl.when(jnp.logical_not(first))
+            @pl.when(group > 1)
             def _():
                 y_to_prev(it, k).start()
 
@@ -516,17 +606,50 @@
                 y_face[it, 0, v, mine, :] = g_inner[it, v, rows, :] + back[v]
             y_to_partner(it, k, True).start()
 
+    def direct_face(it, kind):
+        source, face, side = ((all_b, x_face, 0), (all_g, y_face, 1))[kind]
+        far = 0 if kind == 0 else groups - 1
+        mine = (group > 0) if kind == 0 else (group < groups - 1)
+
+        @pl.when(jnp.logical_not(mine))
+        def _():
+            face[it, side, :, own_rows, :] = face_zero
+
+        @pl.when(mine)
+        def _():
+            direct_copy(it, kind, far, 1).wait_recv()
+            face[it, side, :, own_rows, :] = source[it, far]
+
+        inner = range(1, groups - 1)
+        for i in inner if kind == 0 else reversed(inner):
+            @pl.when((group > i) if kind == 0 else (group < i))
+            def _():
+                direct_copy(it, kind, i, 1).wait_recv()
+                for g, rows in enumerate(steps):
+                    x = [face[it, side, v, own(g), :] for v in range(NV)]
+                    out = times(matrix(all_m.at[kind, i], 0, rows), x)
+                    for v in range(NV):
+                        face[it, side, v, own(g), :] = source[it, i, v, rows, :] + out[v]
+
+    def direct_backward(it):
+        direct_face(it, 1)
+        for k, rows in enumerate(parts):
+            mine = at(own_base + k * PART, PART)
+            y = [y_face[it, 1, v, mine, :] for v in range(NV)]
+            back = times(matrix(mats.at[1], MATS, rows), y)
+            for v in range(NV):
+                y_face[it, 0, v, mine, :] = g_inner[it, v, rows, :] + back[v]
+            y_to_partner(it, k, True).start()
+
     face_zero = jnp.zeros((NV, half, 128), jnp.float32)
 
     @pl.when(first)
     def _():
-        for it in range(ITERS):
-            x_in[it] = face_zero
+        x_in[0] = face_zero
 
     @pl.when(last)
     def _():
-        for it in range(ITERS):
-            y_in[it] = face_zero
+        y_in[0] = face_zero
 
     for it in range(ITERS):
         if it > 0:
@@ -536,6 +659,14 @@
             for copy in sweep_loads:
                 copy.wait()
             lax.fori_loop(0, tiles // 8, transfer, 0)
+            for k in range(3):
+                mats_copy(k).wait_recv()
+            lax.fori_loop(0, half // 8, compose, 0)
+            for kind in range(2):
+                for d in range(2, groups):
+                    send_chip(kind, d, PIECES, True)
+            send_chip(0, 1, PIECES, even)
+            send_chip(1, 1, PIECES, jnp.logical_not(even))
             for copy in drive_loads:
                 copy.wait()
         lane = iota((tiles, 128), 1)
@@ -594,41 +725,69 @@
         zero_down(it, far_base, 2)
         b_to_partner(it).start()
         zero_down(it, own_base, core)
-        if it == 0:
-            for k in range(3):
-                mats_copy(k).wait_recv()
         b_to_partner(it).wait_recv()
         chip_forward(it)
 
-        @pl.when(first)
-        def _():
-            for k in range(len(parts)):
-                x_to_next(it, k, chip_b).start()
+        if it == 0:
+            @pl.when(first)
+            def _():
+                for k in range(len(parts)):
+                    x_to_next(it, k, chip_b).start()
+
+        send_direct(it, 0)
 
         zero_up(it, far_base, 2)
         c_to_partner(it).start()
         zero_up(it, own_base, core)
-        if it == 0:
-            lax.fori_loop(0, half // 8, compose, 0)
         c_to_partner(it).wait_recv()
         chip_backward(it)
-        relay_forward(it)
+        if it == 0:
+            @pl.when(last)
+            def _():
+                wait_mats(0)
+                direct_face(it, 0)
+
+            @pl.when(jnp.logical_not(last))
+            def _():
+                relay_forward(it)
+        else:
+            @pl.when(jnp.logical_not(last))
+            def _():
+                wait_mats(0)
+
+            direct_face(it, 0)
         turn(it)
+        send_direct(it, 1)
         inner_forward(it)
-
-        @pl.when(last)
-        def _():
-            relay_backward(it)
+        if it == 0:
+            @pl.when(last)
+            def _():
+                relay_backward(it)
 
         x_to_partner(it).start()
         true_down(it, own_base)
         x_to_partner(it).wait_recv()
         true_down(it, far_base)
-
-        @pl.when(jnp.logical_not(last))
-        def _():
-            relay_backward(it)
-
+        if it == 0:
+            @pl.when(first)
+            def _():
+                wait_mats(1)
+
+            pass_on(1)
+
+            @pl.when(first)
+            def _():
+                direct_backward(it)
+
+            @pl.when(jnp.logical_not(first | last))
+            def _():
+                relay_backward(it)
+        else:
+            @pl.when(jnp.logical_not(first))
+            def _():
+                wait_mats(1)
+
+            direct_backward(it)
         true_up(it, own_base)
         if it == ITERS - 1:
             for copy in out_copies(0, own_base):
@@ -636,9 +795,30 @@
         for k in range(len(parts)):
             y_to_partner(it, k, False).wait_recv()
         true_up(it, far_base)
+        if it == 0:
+            pass_on(0)
         if it == ITERS - 1:
             for copy in out_copies(1, far_base):
                 copy.start()
+
+    for kind in range(2):
+        @pl.when(passes(kind))
+        def _():
+            for piece in PIECES:
+                pass_copy(kind, piece, group).wait_send()
+
+        for d in range(1, groups):
+            near_by = True if d > 1 else (jnp.logical_not(even) if kind else even)
+
+            @pl.when(chip_to(kind, d) & near_by)
+            def _():
+                for piece in PIECES:
+                    chip_copy(kind, piece, group, d).wait_send()
+
+            for it in range(ITERS):
+                @pl.when(direct_to(it, kind, d))
+                def _():
+                    direct_copy(it, kind, group, d).wait_send()
 
     for k in range(3):
         mats_copy(k).wait_send()
@@ -658,12 +838,15 @@
         for k in range(len(parts)):
             y_to_partner(it, k, True).wait_send()
 
-        @pl.when(jnp.logical_not(last))
+        if it > 0:
+            continue
+
+        @pl.when(group < groups - 2)
         def _():
             for k in range(len(parts)):
                 x_to_next(it, k, x_out).wait_send()
 
-        @pl.when(jnp.logical_not(first))
+        @pl.when(group > 1)
         def _():
             for k in range(len(parts)):
                 y_to_prev(it, k).wait_send()
@@ -695,6 +878,7 @@
 
     full = (NV, planes * tiles, 128)
     half = tiles // 2
+    groups = ns // 2
     f32, bf16 = jnp.float32, jnp.bfloat16
     dma = pltpu.SemaphoreType.DMA
     face = pltpu.VMEM((ITERS, NV, half, 128), f32)
@@ -729,6 +913,9 @@
             pltpu.VMEM((planes, MATS, 8, 128), f32),
             pltpu.VMEM((3, 3 * MATS, half, 128), f32),
             pltpu.VMEM((3 * MATS, half, 128), f32),
+            pltpu.VMEM((2, groups, MATS, half, 128), f32),
+            pltpu.VMEM((ITERS, groups, NV, half, 128), f32),
+            pltpu.VMEM((ITERS, groups, NV, half, 128), f32),
             pltpu.VMEM((ITERS, 3, 2, NV, half, 128), f32),
             face,
             face,
@@ -750,6 +937,10 @@
             dma((3,)),
             dma((ITERS, 3 + 3 * (half // PART))),
             dma((ITERS, 3 + 3 * (half // PART))),
+            dma((2, len(PIECES), groups)),
+            dma((2, len(PIECES), groups)),
+            dma((ITERS, 2, groups)),
+            dma((ITERS, 2, groups)),
         ],
         compiler_params=pltpu.CompilerParams(
             collective_id=0, has_side_effects=True, vmem_limit_bytes=56 * 1024 * 1024

time: 78.4 us -> 70.4 us (0.90)
  Pallas kernels: 73.9 us -> 65.8 us
    pallas_call x1, Pallas kernels: 73.9 us -> 65.8 us  [shards(): pl.pallas_call(functools.partial(kernel, ns, nc, planes, tiles), out_shap...]
where the time goes in v3:
time: 70.4 us; the launch traced here: 70.1 us
  Pallas kernels  65.8 us (93%)
  local copies, waits for them, and re-layouts  3.62 us (5%)
    pallas_call x1, Pallas kernels, shards(): pl.pallas_call(functools.partial(kernel, ns, nc, planes, tiles), out_shap...  65.8 us
    unnamed x4, local copies, waits for them, and re-layouts  3.62 us

profile of v3, /device:TPU:0, one launch (start us, length us, event | category | flops | bytes accessed | tf_op | source)
XLA Modules:
  0.0 70.1 jit_solution(4659259088105803151)
XLA Ops:
  0.6 65.8 %shard_map.131 = (f32[5,64,8,128]{3,2,1,0:T(8,128)}, f32[5,64,8,128]{3,2,1,0:T(8,128)}) custom-call(f32[5,64,8,128]{3,2,1,0:T(8,128)} %bitcast.31, f32[5,64,8,128]{3,2,1,0:T(8,128)} %bitcast.32, f32[5,5,64,8,128]{4,3,2,1,0:T(8,128)} %bitcast.30, f32[5,64,8,128]{3,2,1,0:T(8,128)} %bitcast.33, f32[5,64,8,128]{3,2,1,0:T(8,128)} %bitcast.34, ...), custom_call_target="tpu_custom_call" | custom-call | tf_op jit(solution)/shard_map/pallas_call | solution.py:889
  66.5 0.0 copy-start
  66.5 2.6 %copy.16 = f32[5,8,8192]{2,1,0:T(8,128)} copy(f32[5,8,8192]{2,1,0:T(8,128)} %bitcast.36) | data formatting | bytes 2621440
  69.0 0.0 copy-done
  69.0 1.1 %copy.17 = f32[5,8,8192]{2,1,0:T(8,128)} copy(f32[5,8,8192]{2,1,0:T(8,128)S(1)} %bitcast.35) | data formatting | bytes 2621440
Async XLA Ops:
  66.5 2.6 %copy-start = (f32[5,64,8,128]{3,2,1,0:T(8,128)S(1)}, f32[5,64,8,128]{3,2,1,0:T(8,128)}, u32[]{:S(2)}) copy-start(f32[5,64,8,128]{3,2,1,0:T(8,128)} %get-tuple-element.5) | copy-start | bytes 3932164

commit v4 on v3

--- a/solution.py
+++ b/solution.py
@@ -15,7 +15,6 @@
 PART = 8
 MATS = NV * NV
 PIECES = ((0, 13), (13, 12))
-BATCHES = ((0, 1, 2, 3, 4),)
 MESH = pl.DeviceIdType.MESH
 PAIRS = [(a, b) for a in range(NV) for b in range(a, NV)]
 
@@ -85,8 +84,9 @@
                     inverse.at[pl.ds(top, NV - a), rows_of(i), :],
                 )
             )
+    upper_loads = []
     for i in range(planes):
-        sweep_loads.append(load(upper_h.at[:, :, i, :], upper.at[:, rows_of(i), :]))
+        upper_loads.append(load(upper_h.at[:, :, i, :], upper.at[:, rows_of(i), :]))
     barrier = pltpu.get_barrier_semaphore()
 
     def greet(k, carry):
@@ -376,78 +376,71 @@
         mine = pl.ds(pl.multiple_of(me * SLOT_ROWS, SLOT_ROWS), NV * CAP)
         received[it, mine, :] = outgoing[it, mine, :]
 
-    def transfer(q, carry):
-        each = half // 8
+    each = half // 8
+
+    def place_of(q):
         local = lax.rem(q, each) * 8
         base = jnp.where(q < each, far_base, own_base) + local
-        slot = jnp.where(q < each, 2, core)
-        spot = at(local, 8)
-        for cols in BATCHES:
-            chain = None
-            for i in range(planes):
-                rows = at(i * tiles + base, 8)
-                blocks = block(rows)
-                factor = [lower[v, rows, :] for v in range(NV)]
-                if i == 0:
-                    chain = {b: [blocks[pair(a, b)] * factor[b] for a in range(NV)] for b in cols}
-                else:
-                    chain = {
-                        b: apply(blocks, [factor[v] * chain[b][v] for v in range(NV)]) for b in cols
-                    }
-                if i < planes - 1:
-                    for b in cols:
-                        for a in range(NV):
-                            stage[i, a * NV + b] = chain[b][a]
-            for b in cols:
+        return base, jnp.where(q < each, 2, core), at(local, 8)
+
+    def keep(k, slot, spot, columns):
+        for b in range(NV):
+            for a in range(NV):
+                mats[slot, k * MATS + a * NV + b, spot, :] = columns[b][a]
+
+    def advance(blocks, factor, columns):
+        if columns is None:
+            return [[blocks[pair(a, b)] * factor[b] for a in range(NV)] for b in range(NV)]
+        return [apply(blocks, [factor[v] * columns[b][v] for v in range(NV)]) for b in range(NV)]
+
+    def transfer_a(q, carry):
+        base, slot, spot = place_of(q)
+        chain = None
+        for i in range(planes):
+            rows = at(i * tiles + base, 8)
+            chain = advance(block(rows), [lower[v, rows, :] for v in range(NV)], chain)
+            for b in range(NV):
                 for a in range(NV):
-                    mats[slot, a * NV + b, spot, :] = chain[b][a]
-            both = chain
-            for i in reversed(range(planes - 1)):
-                rows = at(i * tiles + base, 8)
-                blocks = block(rows)
-                factor = [upper[v, rows, :] for v in range(NV)]
-                both = {
-                    b: [
-                        stage[i, a * NV + b] + z
-                        for a, z in enumerate(
-                            apply(blocks, [factor[v] * both[b][v] for v in range(NV)])
-                        )
-                    ]
-                    for b in cols
-                }
-            for b in cols:
-                for a in range(NV):
-                    mats[slot, 2 * MATS + a * NV + b, spot, :] = both[b][a]
-            back = None
-            for i in reversed(range(planes)):
-                rows = at(i * tiles + base, 8)
-                blocks = block(rows)
-                factor = [upper[v, rows, :] for v in range(NV)]
-                if i == planes - 1:
-                    back = {b: [blocks[pair(a, b)] * factor[b] for a in range(NV)] for b in cols}
-                else:
-                    back = {
-                        b: apply(blocks, [factor[v] * back[b][v] for v in range(NV)]) for b in cols
-                    }
-            for b in cols:
-                for a in range(NV):
-                    mats[slot, MATS + a * NV + b, spot, :] = back[b][a]
-
-        @pl.when(q == each - 2)
-        def _():
-            for copy in state_loads:
-                copy.wait()
-            pl.semaphore_wait(barrier, devices - 1)
-            send_donors(0)
+                    stage[i, a * NV + b, at(base, 8), :] = chain[b][a]
+        keep(0, slot, spot, chain)
+        return carry
+
+    def transfer_e(q, carry):
+        base, slot, spot = place_of(q)
+        back = None
+        for i in reversed(range(planes)):
+            rows = at(i * tiles + base, 8)
+            back = advance(block(rows), [upper[v, rows, :] for v in range(NV)], back)
+        keep(1, slot, spot, back)
 
         @pl.when(q == each - 1)
         def _():
-            for k in range(3):
-                mats_copy(k).start()
+            mats_copy(1).start()
 
         return carry
 
-    def compose(q, carry):
+    def transfer_d(q, carry):
+        base, slot, spot = place_of(q)
+        spot_all = at(base, 8)
+        both = [
+            [stage[planes - 1, a * NV + b, spot_all, :] for a in range(NV)] for b in range(NV)
+        ]
+        for i in reversed(range(planes - 1)):
+            rows = at(i * tiles + base, 8)
+            both = advance(block(rows), [upper[v, rows, :] for v in range(NV)], both)
+            both = [
+                [stage[i, a * NV + b, spot_all, :] + both[b][a] for a in range(NV)]
+                for b in range(NV)
+            ]
+        keep(2, slot, spot, both)
+
+        @pl.when(q == each - 1)
+        def _():
+            mats_copy(2).start()
+
+        return carry
+
+    def compose_a(q, carry):
         rows = at(q * 8, 8)
         low_a = matrix(mats.at[0], 0, rows)
         high_a = matrix(mats.at[1], 0, rows)
@@ -455,20 +448,34 @@
             out = times(high_a, column(low_a, b))
             for a in range(NV):
                 comp[a * NV + b, rows, :] = out[a]
+        return carry
+
+    def compose_e(q, carry):
+        rows = at(q * 8, 8)
         low_e = matrix(mats.at[0], MATS, rows)
         high_e = matrix(mats.at[1], MATS, rows)
         for b in range(NV):
             out = times(low_e, column(high_e, b))
             for a in range(NV):
                 comp[MATS + a * NV + b, rows, :] = out[a]
+        return carry
+
+    def compose_d(q, carry):
+        rows = at(q * 8, 8)
+        low_a = matrix(mats.at[0], 0, rows)
+        low_e = matrix(mats.at[0], MATS, rows)
         high_d = matrix(mats.at[1], 2 * MATS, rows)
         for b in range(NV):
-            inner = times(high_d, column(low_a, b))
-            out = times(low_e, inner)
+            out = times(low_e, times(high_d, column(low_a, b)))
             for a in range(NV):
                 k = 2 * MATS + a * NV + b
                 comp[k, rows, :] = mats[0, k, rows, :] + out[a]
         return carry
+
+    def send_matrices(kind):
+        for d in range(2, groups):
+            send_chip(kind, d, PIECES, True)
+        send_chip(kind, 1, PIECES, jnp.logical_not(even) if kind else even)
 
     def zero_down(it, base, slot):
         for g in range(half // STEP):
@@ -658,15 +665,21 @@
             fill_pick()
             for copy in sweep_loads:
                 copy.wait()
-            lax.fori_loop(0, tiles // 8, transfer, 0)
-            for k in range(3):
-                mats_copy(k).wait_recv()
-            lax.fori_loop(0, half // 8, compose, 0)
-            for kind in range(2):
-                for d in range(2, groups):
-                    send_chip(kind, d, PIECES, True)
-            send_chip(0, 1, PIECES, even)
-            send_chip(1, 1, PIECES, jnp.logical_not(even))
+            lax.fori_loop(0, tiles // 8, transfer_a, 0)
+            for copy in state_loads:
+                copy.wait()
+            pl.semaphore_wait(barrier, devices - 1)
+            mats_copy(0).start()
+            send_donors(0)
+            mats_copy(0).wait_recv()
+            lax.fori_loop(0, each, compose_a, 0)
+            send_matrices(0)
+            for copy in upper_loads:
+                copy.wait()
+            lax.fori_loop(0, tiles // 8, transfer_e, 0)
+            mats_copy(1).wait_recv()
+            lax.fori_loop(0, each, compose_e, 0)
+            send_matrices(1)
             for copy in drive_loads:
                 copy.wait()
         lane = iota((tiles, 128), 1)
@@ -739,6 +752,14 @@
         zero_up(it, far_base, 2)
         c_to_partner(it).start()
         zero_up(it, own_base, core)
+        if it == 0:
+            @pl.when((group > 0) & (group < groups - 2))
+            def _():
+                relay_forward(it)
+
+            lax.fori_loop(0, tiles // 8, transfer_d, 0)
+            mats_copy(2).wait_recv()
+            lax.fori_loop(0, each, compose_d, 0)
         c_to_partner(it).wait_recv()
         chip_backward(it)
         if it == 0:
@@ -747,7 +768,7 @@
                 wait_mats(0)
                 direct_face(it, 0)
 
-            @pl.when(jnp.logical_not(last))
+            @pl.when(first | (group == groups - 2))
             def _():
                 relay_forward(it)
         else:
@@ -910,7 +931,7 @@
             pltpu.VMEM((3 * slots, NV * 128), bf16),
             pltpu.VMEM((ITERS, 2, NV, planes, 128), f32),
             pltpu.VMEM((ITERS, 2, NV, planes, 128), f32),
-            pltpu.VMEM((planes, MATS, 8, 128), f32),
+            pltpu.VMEM((planes, MATS, tiles, 128), f32),
             pltpu.VMEM((3, 3 * MATS, half, 128), f32),
             pltpu.VMEM((3 * MATS, half, 128), f32),
             pltpu.VMEM((2, groups, MATS, half, 128), f32),

time: 70.4 us -> 65.9 us (0.936)
  Pallas kernels: 65.8 us -> 61.2 us
    pallas_call x1, Pallas kernels: 65.8 us -> 61.2 us  [shards(): pl.pallas_call(functools.partial(kernel, ns, nc, planes, tiles), out_shap...]
where the time goes in v4:
time: 65.9 us; the launch traced here: 65.5 us
  Pallas kernels  61.2 us (93%)
  local copies, waits for them, and re-layouts  3.62 us (5%)
    pallas_call x1, Pallas kernels, shards(): pl.pallas_call(functools.partial(kernel, ns, nc, planes, tiles), out_shap...  61.2 us
    unnamed x4, local copies, waits for them, and re-layouts  3.62 us

profile of v4, /device:TPU:0, one launch (start us, length us, event | category | flops | bytes accessed | tf_op | source)
XLA Modules:
  0.0 65.5 jit_solution(9367900428628645759)
XLA Ops:
  0.6 61.2 %shard_map.131 = (f32[5,64,8,128]{3,2,1,0:T(8,128)}, f32[5,64,8,128]{3,2,1,0:T(8,128)}) custom-call(f32[5,64,8,128]{3,2,1,0:T(8,128)} %bitcast.31, f32[5,64,8,128]{3,2,1,0:T(8,128)} %bitcast.32, f32[5,5,64,8,128]{4,3,2,1,0:T(8,128)} %bitcast.30, f32[5,64,8,128]{3,2,1,0:T(8,128)} %bitcast.33, f32[5,64,8,128]{3,2,1,0:T(8,128)} %bitcast.34, ...), custom_call_target="tpu_custom_call" | custom-call | tf_op jit(solution)/shard_map/pallas_call | solution.py:910
  61.8 0.0 copy-start
  61.9 2.6 %copy.16 = f32[5,8,8192]{2,1,0:T(8,128)} copy(f32[5,8,8192]{2,1,0:T(8,128)} %bitcast.36) | data formatting | bytes 2621440
  64.4 0.0 copy-done
  64.4 1.1 %copy.17 = f32[5,8,8192]{2,1,0:T(8,128)} copy(f32[5,8,8192]{2,1,0:T(8,128)S(1)} %bitcast.35) | data formatting | bytes 2621440
Async XLA Ops:
  61.8 2.6 %copy-start = (f32[5,64,8,128]{3,2,1,0:T(8,128)S(1)}, f32[5,64,8,128]{3,2,1,0:T(8,128)}, u32[]{:S(2)}) copy-start(f32[5,64,8,128]{3,2,1,0:T(8,128)} %get-tuple-element.5) | copy-start | bytes 3932164

commit v5 on v4

--- a/solution.py
+++ b/solution.py
@@ -169,6 +169,7 @@
         return other_group * 2 + (1 - core if across else core)
 
     partner = member(group, True)
+    parts = [pl.ds(k * PART, PART) for k in range(half // PART)]
 
     def face_copy(it, kind, way, source, target, to):
         return pltpu.make_async_remote_copy(
@@ -255,14 +256,15 @@
             for piece in pieces:
                 chip_copy(kind, piece, group, d).start()
 
-    def direct_copy(it, kind, sender, d):
+    def direct_copy(it, kind, sender, d, k):
+        rows = parts[k]
         source, target = ((chip_b, all_b), (g_own, all_g))[kind]
         away = d if kind == 0 else -d
         return pltpu.make_async_remote_copy(
-            src_ref=source.at[it],
-            dst_ref=target.at[it, sender],
-            send_sem=dsend.at[it, kind, d],
-            recv_sem=drecv.at[it, kind, sender],
+            src_ref=source.at[it, :, rows, :],
+            dst_ref=target.at[it, sender, :, rows, :],
+            send_sem=dsend.at[it, kind, d, k],
+            recv_sem=drecv.at[it, kind, sender, k],
             device_id=(member(group + away, d % 2 == 1), c),
             device_id_type=MESH,
         )
@@ -272,19 +274,17 @@
             return (group + d == groups - 1) if kind == 0 else (group == d)
         return (group + d < groups) if kind == 0 else (group >= d)
 
-    def send_direct(it, kind):
+    def send_direct(it, kind, k):
         for d in reversed(range(1, groups)):
             @pl.when(direct_to(it, kind, d))
             def _():
-                direct_copy(it, kind, group, d).start()
+                direct_copy(it, kind, group, d, k).start()
 
     def b_to_partner(it):
         return face_copy(it, 0, 0, zero.at[it, 2, 0], zero.at[it, core, 0], partner)
 
     def c_to_partner(it):
         return face_copy(it, 1, 1, zero.at[it, 2, 1], zero.at[it, core, 1], partner)
-
-    parts = [pl.ds(k * PART, PART) for k in range(half // PART)]
 
     def x_to_next(it, k, source):
         rows = parts[k]
@@ -403,6 +403,15 @@
                 for a in range(NV):
                     stage[i, a * NV + b, at(base, 8), :] = chain[b][a]
         keep(0, slot, spot, chain)
+
+        @pl.when(q == each - 1)
+        def _():
+            for copy in state_loads:
+                copy.wait()
+            pl.semaphore_wait(barrier, devices - 1)
+            send_donors(0)
+            mats_copy(0).start()
+
         return carry
 
     def transfer_e(q, carry):
@@ -574,12 +583,12 @@
             def _():
                 x_to_next(it, k, x_out).start()
 
-    def turn(it):
-        for g, rows in enumerate(steps):
-            x = [x_face[it, 0, v, own(g), :] for v in range(NV)]
-            out = times(matrix(comp, 2 * MATS, rows), x)
-            for v in range(NV):
-                g_own[it, v, rows, :] = chip_c[it, v, rows, :] + out[v]
+    def turn(it, k):
+        rows = parts[k]
+        x = [x_face[it, 0, v, at(own_base + k * PART, PART), :] for v in range(NV)]
+        out = times(matrix(comp, 2 * MATS, rows), x)
+        for v in range(NV):
+            g_own[it, v, rows, :] = chip_c[it, v, rows, :] + out[v]
 
     def inner_forward(it):
         for g, rows in enumerate(steps):
@@ -613,34 +622,40 @@
                 y_face[it, 0, v, mine, :] = g_inner[it, v, rows, :] + back[v]
             y_to_partner(it, k, True).start()
 
-    def direct_face(it, kind):
+    def direct_face(it, kind, k):
         source, face, side = ((all_b, x_face, 0), (all_g, y_face, 1))[kind]
         far = 0 if kind == 0 else groups - 1
         mine = (group > 0) if kind == 0 else (group < groups - 1)
+        rows, spot = parts[k], at(own_base + k * PART, PART)
 
         @pl.when(jnp.logical_not(mine))
         def _():
-            face[it, side, :, own_rows, :] = face_zero
+            face[it, side, :, spot, :] = jnp.zeros((NV, PART, 128), jnp.float32)
 
         @pl.when(mine)
         def _():
-            direct_copy(it, kind, far, 1).wait_recv()
-            face[it, side, :, own_rows, :] = source[it, far]
+            direct_copy(it, kind, far, 1, k).wait_recv()
+            face[it, side, :, spot, :] = source[it, far, :, rows, :]
 
         inner = range(1, groups - 1)
         for i in inner if kind == 0 else reversed(inner):
             @pl.when((group > i) if kind == 0 else (group < i))
             def _():
-                direct_copy(it, kind, i, 1).wait_recv()
-                for g, rows in enumerate(steps):
-                    x = [face[it, side, v, own(g), :] for v in range(NV)]
-                    out = times(matrix(all_m.at[kind, i], 0, rows), x)
-                    for v in range(NV):
-                        face[it, side, v, own(g), :] = source[it, i, v, rows, :] + out[v]
+                direct_copy(it, kind, i, 1, k).wait_recv()
+                x = [face[it, side, v, spot, :] for v in range(NV)]
+                out = times(matrix(all_m.at[kind, i], 0, rows), x)
+                for v in range(NV):
+                    face[it, side, v, spot, :] = source[it, i, v, rows, :] + out[v]
+
+    def direct_forward(it):
+        for k in range(len(parts)):
+            direct_face(it, 0, k)
+            turn(it, k)
+            send_direct(it, 1, k)
 
     def direct_backward(it):
-        direct_face(it, 1)
         for k, rows in enumerate(parts):
+            direct_face(it, 1, k)
             mine = at(own_base + k * PART, PART)
             y = [y_face[it, 1, v, mine, :] for v in range(NV)]
             back = times(matrix(mats.at[1], MATS, rows), y)
@@ -666,11 +681,6 @@
             for copy in sweep_loads:
                 copy.wait()
             lax.fori_loop(0, tiles // 8, transfer_a, 0)
-            for copy in state_loads:
-                copy.wait()
-            pl.semaphore_wait(barrier, devices - 1)
-            mats_copy(0).start()
-            send_donors(0)
             mats_copy(0).wait_recv()
             lax.fori_loop(0, each, compose_a, 0)
             send_matrices(0)
@@ -747,7 +757,8 @@
                 for k in range(len(parts)):
                     x_to_next(it, k, chip_b).start()
 
-        send_direct(it, 0)
+        for k in range(len(parts)):
+            send_direct(it, 0, k)
 
         zero_up(it, far_base, 2)
         c_to_partner(it).start()
@@ -766,19 +777,23 @@
             @pl.when(last)
             def _():
                 wait_mats(0)
-                direct_face(it, 0)
+                direct_forward(it)
 
             @pl.when(first | (group == groups - 2))
             def _():
                 relay_forward(it)
+
+            @pl.when(jnp.logical_not(last))
+            def _():
+                for k in range(len(parts)):
+                    turn(it, k)
+                    send_direct(it, 1, k)
         else:
             @pl.when(jnp.logical_not(last))
             def _():
                 wait_mats(0)
 
-            direct_face(it, 0)
-        turn(it)
-        send_direct(it, 1)
+            direct_forward(it)
         inner_forward(it)
         if it == 0:
             @pl.when(last)
@@ -839,7 +854,8 @@
             for it in range(ITERS):
                 @pl.when(direct_to(it, kind, d))
                 def _():
-                    direct_copy(it, kind, group, d).wait_send()
+                    for k in range(len(parts)):
+                        direct_copy(it, kind, group, d, k).wait_send()
 
     for k in range(3):
         mats_copy(k).wait_send()
@@ -960,8 +976,8 @@
             dma((ITERS, 3 + 3 * (half // PART))),
             dma((2, len(PIECES), groups)),
             dma((2, len(PIECES), groups)),
-            dma((ITERS, 2, groups)),
-            dma((ITERS, 2, groups)),
+            dma((ITERS, 2, groups, half // PART)),
+            dma((ITERS, 2, groups, half // PART)),
         ],
         compiler_params=pltpu.CompilerParams(
             collective_id=0, has_side_effects=True, vmem_limit_bytes=56 * 1024 * 1024

time: 65.9 us -> 64.5 us (0.979)
  Pallas kernels: 61.2 us -> 60 us
    pallas_call x1, Pallas kernels: 61.2 us -> 60 us  [shards(): pl.pallas_call(functools.partial(kernel, ns, nc, planes, tiles), out_shap...]
where the time goes in v5:
time: 64.5 us; the launch traced here: 64.3 us
  Pallas kernels  60 us (93%)
  local copies, waits for them, and re-layouts  3.62 us (6%)
  between operations  0.65 us (1%)
    pallas_call x1, Pallas kernels, shards(): pl.pallas_call(functools.partial(kernel, ns, nc, planes, tiles), out_shap...  60 us
    unnamed x4, local copies, waits for them, and re-layouts  3.62 us

profile of v5, /device:TPU:0, one launch (start us, length us, event | category | flops | bytes accessed | tf_op | source)
XLA Modules:
  0.0 64.3 jit_solution(9640169846763575262)
XLA Ops:
  0.6 60.0 %shard_map.131 = (f32[5,64,8,128]{3,2,1,0:T(8,128)}, f32[5,64,8,128]{3,2,1,0:T(8,128)}) custom-call(f32[5,64,8,128]{3,2,1,0:T(8,128)} %bitcast.31, f32[5,64,8,128]{3,2,1,0:T(8,128)} %bitcast.32, f32[5,5,64,8,128]{4,3,2,1,0:T(8,128)} %bitcast.30, f32[5,64,8,128]{3,2,1,0:T(8,128)} %bitcast.33, f32[5,64,8,128]{3,2,1,0:T(8,128)} %bitcast.34, ...), custom_call_target="tpu_custom_call" | custom-call | tf_op jit(solution)/shard_map/pallas_call | solution.py:926
  60.7 0.0 copy-start
  60.7 2.6 %copy.16 = f32[5,8,8192]{2,1,0:T(8,128)} copy(f32[5,8,8192]{2,1,0:T(8,128)} %bitcast.36) | data formatting | bytes 2621440
  63.3 0.0 copy-done
  63.3 1.1 %copy.17 = f32[5,8,8192]{2,1,0:T(8,128)} copy(f32[5,8,8192]{2,1,0:T(8,128)S(1)} %bitcast.35) | data formatting | bytes 2621440
Async XLA Ops:
  60.7 2.6 %copy-start = (f32[5,64,8,128]{3,2,1,0:T(8,128)S(1)}, f32[5,64,8,128]{3,2,1,0:T(8,128)}, u32[]{:S(2)}) copy-start(f32[5,64,8,128]{3,2,1,0:T(8,128)} %get-tuple-element.5) | copy-start | bytes 3932164
